TPU v7x, 32 devices: a whole 2x2x4 slice. The times are simulated.
32 devices in a mesh: dp: 2 (over y), row: 4 (over z), col: 4 (over x, core).
Axes of the slice: x: 2, y: 2, z: 4, core: 2. Of those that a mesh axis runs over, the one named last changes fastest.
Arguments:
- tokens: bfloat16 [8192, 1152], P(('dp', 'col'), 'row'), may hold values from -1 to 3
- class_ids: int32 [8], P('dp'), may hold values from 0 to 999
- time_ids: int32 [8], P('dp'), may hold values from 0 to 999
- class_table: bfloat16 [1000, 1152], P(None, 'col'), may hold values from -6 to 6
- adaptive_norm_weight: bfloat16 [1152, 6, 1152], P('col', None, 'row'), may hold values from -0.1875 to 0.1875
- adaptive_norm_bias: bfloat16 [6, 1152], P(None, 'row'), may hold values from -3 to 3
- query_key_value_weight: bfloat16 [1152, 3, 1152], P('row', None, 'col'), may hold values from -0.1875 to 0.1875
- query_value_bias: bfloat16 [2, 1152], P(None, 'col'), may hold values from -3 to 3
- w_out: bfloat16 [1152, 1152], P('col', 'row'), may hold values from -1.5 to 1.5
- out_bias: bfloat16 [1152], P('row'), may hold values from -3 to 3
- w_fc1: bfloat16 [1152, 4608], P('row', 'col'), may hold values from -0.1875 to 0.1875
- fc1_bias: bfloat16 [4608], P('col'), may hold values from -3 to 3
- w_fc2: bfloat16 [4608, 1152], P('col', 'row'), may hold values from -0.09375 to 0.09375
- fc2_bias: bfloat16 [1152], P('row'), may hold values from -3 to 3
- cotangent: bfloat16 [8192, 1152], P(('dp', 'col'), 'row'), may hold values from -6 to 6
Outputs:
- mixed: bfloat16 [8192, 1152], P(('dp', 'col'), 'row')
- d_tokens: float32 [8192, 1152], P(('dp', 'col'), 'row')
- d_class_table: float32 [1000, 1152], P(None, 'col')
- d_ada_weight: float32 [1152, 6, 1152], P('col', None, 'row')
- d_ada_bias: float32 [6, 1152], P(None, 'row')
- d_w_qkv: float32 [1152, 3, 1152], P('row', None, 'col')
- d_query_value_bias: float32 [2, 1152], P(None, 'col')
- d_w_out: float32 [1152, 1152], P('col', 'row')
- d_out_bias: float32 [1152], P('row')
- d_w_fc1: float32 [1152, 4608], P('row', 'col')
- d_fc1_bias: float32 [4608], P('col')
- d_w_fc2: float32 [4608, 1152], P('col', 'row')
- d_fc2_bias: float32 [1152], P('row')
All inputs are finite; a program needn't handle non-finite values.
Results may differ from a plain program's by a relative error of at most 0.014.
The roundings to bfloat16 on the way count: a program that leaves them out, or rounds other values in their place, can miss the bound.
Values may be sent and summed in bfloat16 or wider, within the bound.
A program may use at most 192 MiB of HBM per device.

v0:
```python
from functools import partial
import math

import jax
import jax.numpy as jnp
from jax import lax
from jax.sharding import PartitionSpec as P

D = 1152
HD = 72
NCLS = 1000
SEQ = 1024
LAT_DEV = 4


def time_embedding(time_ids):
    half_width = D // 2
    freqs = jnp.exp(-math.log(10000.0) * jnp.arange(half_width, dtype=jnp.float32) / half_width)
    angles = time_ids.astype(jnp.float32)[:, None] * freqs[None, :]
    return jnp.concatenate([jnp.cos(angles), jnp.sin(angles)], axis=-1)


def contract_with(left, weight, contract):
    return lax.dot_general(
        left, weight, (((1,), (contract,)), ((), ())), preferred_element_type=jnp.float32
    )


def through_rows(source, weight, contract):
    gathered = lax.all_gather(source, "col", axis=0, tiled=True)
    share = gathered.shape[0] // lax.axis_size("row")

    def partial_term(start, count):
        return contract_with(gathered, weight, contract)

    return (
        lax.psum_scatter(
            partial_term(jnp.int32(0), share * lax.axis_size("row")),
            "row",
            scatter_dimension=0,
            tiled=True,
        ),
        gathered,
    )


def through_cols(source, weight, contract):
    gathered = lax.all_gather(source, "row", axis=0, tiled=True)
    share = gathered.shape[0] // lax.axis_size("col")

    def partial_term(start, count):
        piece = lax.dynamic_slice_in_dim(gathered, start, count, 0)
        return contract_with(piece, weight, contract)

    return (
        lax.psum_scatter(
            partial_term(jnp.int32(0), share * lax.axis_size("col")),
            "col",
            scatter_dimension=0,
            tiled=True,
        ),
        gathered,
    )


def weight_grad(left, right):
    return lax.dot_general(
        left, right, (((0,), (0,)), ((), ())), preferred_element_type=jnp.float32
    )


def grid_grad(kept, back_kept):
    return weight_grad(kept, back_kept)


def feature_sums(parts):
    return lax.psum(parts, "row")


def normalize(values):
    total = feature_sums((jnp.sum(values, axis=-1),))[0]
    centred = values - (total / D)[..., None]
    spread = feature_sums((jnp.sum(centred * centred, axis=-1),))[0] / D
    inv_std = lax.rsqrt(spread + 1e-06)
    return (centred * inv_std[..., None], inv_std)


def norm_back(d_input, normed, inv_std, scale_row):
    d_normed = d_input * (1.0 + scale_row[:, None, :])
    first_sum, cross_sum = feature_sums(
        (jnp.sum(d_normed, axis=-1), jnp.sum(d_normed * normed, axis=-1))
    )
    return inv_std[..., None] * (
        d_normed - first_sum[..., None] / D - normed * cross_sum[..., None] / D
    )


def attend(block):
    queries, keys, values = block
    scores = jnp.einsum("qhe,khe->hqk", queries, keys, preferred_element_type=jnp.float32) * (
        1.0 / math.sqrt(HD)
    )
    biggest = jnp.max(scores, axis=-1, keepdims=True)
    expo = jnp.exp(scores - biggest)
    totals = jnp.sum(expo, axis=-1, keepdims=True)
    weights = (expo / totals).astype(jnp.bfloat16)
    result = jnp.einsum("hqk,khe->qhe", weights, values, preferred_element_type=jnp.float32)
    return (result.reshape(SEQ, -1), (biggest + jnp.log(totals))[..., 0])


def attend_back(block):
    queries, keys, values, log_totals, d_result = block
    scale = 1.0 / math.sqrt(HD)
    scores = jnp.einsum("qhe,khe->hqk", queries, keys, preferred_element_type=jnp.float32) * scale
    probs = jnp.exp(scores - log_totals[..., None])
    d_values = jnp.einsum(
        "hqk,qhe->khe", probs.astype(jnp.bfloat16), d_result, preferred_element_type=jnp.float32
    )
    d_probs = jnp.einsum("qhe,khe->hqk", d_result, values, preferred_element_type=jnp.float32)
    inner = jnp.sum(probs * d_probs, axis=-1, keepdims=True)
    d_scores = (probs * (d_probs - inner)).astype(jnp.bfloat16)
    d_queries = (
        jnp.einsum("hqk,khe->qhe", d_scores, keys, preferred_element_type=jnp.float32) * scale
    )
    d_keys = (
        jnp.einsum("hqk,qhe->khe", d_scores, queries, preferred_element_type=jnp.float32) * scale
    )
    return jnp.stack(
        [d_queries.reshape(SEQ, -1), d_keys.reshape(SEQ, -1), d_values.reshape(SEQ, -1)], axis=1
    )


def per_device(
    tokens,
    class_ids,
    time_ids,
    class_table,
    adaptive_norm_weight,
    adaptive_norm_bias,
    query_key_value_weight,
    query_value_bias,
    w_out,
    out_bias,
    w_fc1,
    fc1_bias,
    w_fc2,
    fc2_bias,
    cotangent,
):
    highest_precision = lax.Precision.HIGHEST
    col_width = class_table.shape[1]
    row_width = tokens.shape[1]
    local_lats = LAT_DEV // lax.axis_size("col")
    attn_lats = LAT_DEV // lax.axis_size("row")
    local_rows = local_lats * SEQ
    heads_here = col_width // HD
    onehot = (class_ids[:, None] == jnp.arange(NCLS, dtype=jnp.int32)[None, :]).astype(jnp.bfloat16)
    labels = jnp.dot(onehot, class_table, preferred_element_type=jnp.float32)
    timing = lax.dynamic_slice_in_dim(
        time_embedding(time_ids), lax.axis_index("col") * col_width, col_width, 1
    )
    condition = labels + timing
    silu_condition = jax.nn.silu(condition).astype(jnp.bfloat16)
    modulation_pieces = jnp.einsum(
        "au,uop->aop", silu_condition, adaptive_norm_weight, preferred_element_type=jnp.float32
    )
    modulation_vectors = (
        lax.psum_scatter(modulation_pieces, "col", scatter_dimension=0, tiled=True)
        + adaptive_norm_bias.astype(jnp.float32)[None]
    )

    def rows_of(index):
        return modulation_vectors[:, index][:, None, :]

    latent_tokens = tokens.astype(jnp.float32).reshape(local_lats, SEQ, row_width)
    normed_first, inv_first = normalize(latent_tokens)
    residual_input_first = (
        (normed_first * (1.0 + rows_of(1)) + rows_of(0))
        .astype(jnp.bfloat16)
        .reshape(local_rows, row_width)
    )
    qkv_flat = query_key_value_weight.reshape(row_width, 3 * col_width)
    projected_condition, first_kept = through_rows(residual_input_first, qkv_flat, 0)
    bias_broadcast_rows = query_value_bias.astype(jnp.float32)
    bias_full = jnp.stack(
        [bias_broadcast_rows[0], jnp.zeros_like(bias_broadcast_rows[0]), bias_broadcast_rows[1]]
    )
    attn_rows = projected_condition.shape[0]
    qkv_values = (projected_condition.reshape(attn_rows, 3, col_width) + bias_full[None]).astype(
        jnp.bfloat16
    )
    split = qkv_values.reshape(attn_lats, SEQ, 3, heads_here, HD)
    queries, keys, values = (split[:, :, 0], split[:, :, 1], split[:, :, 2])
    attended, log_totals = lax.map(attend, (queries, keys, values))
    attended = attended.reshape(attn_rows, col_width).astype(jnp.bfloat16)
    branch_sum, attended_kept = through_cols(attended, w_out, 0)
    branch = (branch_sum + out_bias.astype(jnp.float32)).reshape(local_lats, SEQ, row_width)
    middle = latent_tokens + rows_of(2) * branch
    normed_second, inv_second = normalize(middle)
    second_input = (
        (normed_second * (1.0 + rows_of(4)) + rows_of(3))
        .astype(jnp.bfloat16)
        .reshape(local_rows, row_width)
    )
    hidden_sum, second_kept = through_rows(second_input, w_fc1, 0)
    hidden = hidden_sum + fc1_bias.astype(jnp.float32)
    gelu_fn = partial(jax.nn.gelu, approximate=True)
    activ = gelu_fn(hidden).astype(jnp.bfloat16)
    feed_sum, activ_kept = through_cols(activ, w_fc2, 0)
    feed = (feed_sum + fc2_bias.astype(jnp.float32)).reshape(local_lats, SEQ, row_width)
    mixed = (middle + rows_of(5) * feed).astype(jnp.bfloat16).reshape(local_rows, row_width)
    upstream = cotangent.astype(jnp.float32).reshape(local_lats, SEQ, row_width)
    d_feed = (upstream * rows_of(5)).astype(jnp.bfloat16).reshape(local_rows, row_width)
    d_fc2_bias = jnp.sum(d_feed.astype(jnp.float32), axis=0)
    d_activ, d_feed_kept = through_rows(d_feed, w_fc2, 1)
    d_w_fc2 = grid_grad(activ_kept, d_feed_kept)
    d_hidden = jax.vjp(gelu_fn, hidden)[1](d_activ)[0].astype(jnp.bfloat16)
    d_fc1_bias = jnp.sum(d_hidden.astype(jnp.float32), axis=0)
    d_second, d_hidden_kept = through_cols(d_hidden, w_fc1, 1)
    d_w_fc1 = grid_grad(second_kept, d_hidden_kept)
    d_second = d_second.reshape(local_lats, SEQ, row_width)
    d_middle = upstream + norm_back(d_second, normed_second, inv_second, modulation_vectors[:, 4])
    d_branch = (d_middle * rows_of(2)).astype(jnp.bfloat16).reshape(local_rows, row_width)
    d_out_bias = jnp.sum(d_branch.astype(jnp.float32), axis=0)
    d_attended, d_branch_kept = through_rows(d_branch, w_out, 1)
    d_w_out = grid_grad(attended_kept, d_branch_kept)
    d_attended = d_attended.astype(jnp.bfloat16).reshape(attn_lats, SEQ, heads_here, HD)
    d_qkv = lax.map(attend_back, (queries, keys, values, log_totals, d_attended))
    d_qkv = d_qkv.reshape(attn_rows, 3, col_width).astype(jnp.bfloat16)
    d_qkv_wide = d_qkv.astype(jnp.float32)
    d_query_value_bias = jnp.stack(
        [jnp.sum(d_qkv_wide[:, 0], axis=0), jnp.sum(d_qkv_wide[:, 2], axis=0)]
    )
    d_qkv_flat = d_qkv.reshape(attn_rows, 3 * col_width)
    d_first, d_qkv_kept = through_cols(d_qkv_flat, qkv_flat, 1)
    d_w_qkv = grid_grad(first_kept, d_qkv_kept).reshape(row_width, 3, col_width)
    d_first = d_first.reshape(local_lats, SEQ, row_width)
    d_tokens = (
        d_middle + norm_back(d_first, normed_first, inv_first, modulation_vectors[:, 1])
    ).reshape(local_rows, row_width)
    d_mod_local = jnp.stack(
        [
            jnp.sum(d_first, axis=1),
            jnp.sum(d_first * normed_first, axis=1),
            jnp.sum(d_middle * branch, axis=1),
            jnp.sum(d_second, axis=1),
            jnp.sum(d_second * normed_second, axis=1),
            jnp.sum(upstream * feed, axis=1),
        ],
        axis=1,
    )
    modulation_gradient = lax.all_gather(d_mod_local, "col", axis=0, tiled=True)
    d_ada_bias = jnp.sum(modulation_gradient, axis=0)
    d_ada_weight = jnp.einsum(
        "qk,qfb->kfb",
        silu_condition.astype(jnp.float32),
        modulation_gradient,
        precision=highest_precision,
    )
    d_activated = jnp.einsum(
        "qnp,unp->qu",
        modulation_gradient,
        adaptive_norm_weight.astype(jnp.float32),
        precision=highest_precision,
    )
    d_condition = jax.vjp(jax.nn.silu, condition)[1](d_activated)[0]
    d_table = lax.dot_general(
        onehot.astype(jnp.float32),
        d_condition,
        (((0,), (0,)), ((), ())),
        precision=highest_precision,
    )
    d_w_qkv, d_w_out, d_w_fc1, d_w_fc2, d_ada_weight, d_ada_bias = lax.psum(
        (d_w_qkv, d_w_out, d_w_fc1, d_w_fc2, d_ada_weight, d_ada_bias), "dp"
    )
    d_table, d_query_value_bias, d_fc1_bias = lax.psum(
        (d_table, d_query_value_bias, d_fc1_bias), ("dp", "row")
    )
    d_out_bias, d_fc2_bias = lax.psum((d_out_bias, d_fc2_bias), ("dp", "col"))
    return (
        mixed,
        d_tokens,
        d_table,
        d_ada_weight,
        d_ada_bias,
        d_w_qkv,
        d_query_value_bias,
        d_w_out,
        d_out_bias,
        d_w_fc1,
        d_fc1_bias,
        d_w_fc2,
        d_fc2_bias,
    )


def solution(mesh):
    return jax.shard_map(
        per_device,
        mesh=mesh,
        in_specs=(
            P(("dp", "col"), "row"),
            P("dp"),
            P("dp"),
            P(None, "col"),
            P("col", None, "row"),
            P(None, "row"),
            P("row", None, "col"),
            P(None, "col"),
            P("col", "row"),
            P("row"),
            P("row", "col"),
            P("col"),
            P("col", "row"),
            P("row"),
            P(("dp", "col"), "row"),
        ),
        out_specs=(
            P(("dp", "col"), "row"),
            P(("dp", "col"), "row"),
            P(None, "col"),
            P("col", None, "row"),
            P(None, "row"),
            P("row", None, "col"),
            P(None, "col"),
            P("col", "row"),
            P("row"),
            P("row", "col"),
            P("col"),
            P("col", "row"),
            P("row"),
        ),
        check_vma=False,
    )
```

profile of v0, /device:TPU:0, one launch (start us, length us, event | category | flops | bytes accessed | tf_op | source)
XLA Modules:
  0.0 2219.5 jit_solution(6381276958604971934)
XLA Ops:
  9.3 13.6 psum.133
  24.1 8.4 psum.134
  35.0 10.5 all-reduce
  48.4 23.6 %all-gather.9.cloned.1.call-done = bf16[4096,288]{0,1:T(8,128)(2,1)} async-done(((bf16[1024,288]{0,1:T(8,128)(2,1)}), bf16[4096,288]{0,1:T(8,128)(2,1)}) %all-gather.9.cloned.1.call-update) | async-done | bytes 2359312 | tf_op jit(solution)/shard_map/all_gather | solution.py:30
  72.0 8.7 fusion.70
  81.6 236.6 %reduce-scatter.10.cloned.1.call-done = f32[1024,864]{0,1:T(8,128)} async-done(((f32[4096,864]{0,1:T(8,128)}), f32[1024,864]{0,1:T(8,128)}) %reduce-scatter.10.cloned.1.call-update) | async-done | bytes 3538960 | tf_op jit(solution)/shard_map/reduce_scatter | solution.py:37
  318.2 2.3 add_convert_fusion
  320.4 8.2 multiply_reduce_fusion.1
  328.6 8.5 fusion
  337.2 8.5 fusion.18
  346.2 51.1 %all-gather.11.cloned.1.call-done = bf16[4096,288]{0,1:T(8,128)(2,1)} async-done(((bf16[1024,288]{0,1:T(8,128)(2,1)}), bf16[4096,288]{0,1:T(8,128)(2,1)}) %all-gather.11.cloned.1.call-update) | async-done | bytes 2359312 | tf_op jit(solution)/shard_map/all_gather | solution.py:48
  397.3 5.2 fusion.61
  404.7 44.7 %reduce-scatter.12.cloned.1.call-done = f32[1024,288]{0,1:T(8,128)} async-done(((f32[4096,288]{0,1:T(8,128)}), f32[1024,288]{0,1:T(8,128)}) %reduce-scatter.12.cloned.1.call-update) | async-done | bytes 1179664 | tf_op jit(solution)/shard_map/reduce_scatter | solution.py:56
  449.4 1.5 fusion.59
  450.9 11.7 psum.135
  462.8 8.4 psum.136
  472.3 3.2 all-gather.17.cloned.1.call-done
  475.6 11.0 fusion.64
  486.7 15.1 all-gather.13.cloned.1.call-done
  501.7 11.1 fusion.62
  513.5 304.5 %reduce-scatter.18.cloned.1.call-done = f32[1024,1152]{1,0:T(8,128)} async-done(((f32[4096,1152]{1,0:T(8,128)}), f32[1024,1152]{1,0:T(8,128)}) %reduce-scatter.18.cloned.1.call-update) | async-done | bytes 4718608 | tf_op jit(solution)/shard_map/reduce_scatter | solution.py:37
  818.0 317.3 %reduce-scatter.14.cloned.1.call-done = f32[1024,1152]{1,0:T(8,128)} async-done(((f32[4096,1152]{1,0:T(8,128)}), f32[1024,1152]{1,0:T(8,128)}) %reduce-scatter.14.cloned.1.call-update) | async-done | bytes 4718608 | tf_op jit(solution)/shard_map/reduce_scatter | solution.py:37
  1135.3 7.5 convert_reduce_fusion
  1143.7 167.2 %all-gather.19.cloned.1.call-done = bf16[4096,1152]{1,0:T(8,128)(2,1)} async-done(((bf16[1024,1152]{1,0:T(8,128)(2,1)}), bf16[4096,1152]{1,0:T(8,128)(2,1)}) %all-gather.19.cloned.1.call-update) | async-done | bytes 9437200 | tf_op jit(solution)/shard_map/all_gather | solution.py:48
  1310.8 9.4 fusion.65
  1320.3 157.0 %all-gather.15.cloned.1.call-done = bf16[4096,1152]{1,0:T(8,128)(2,1)} async-done(((bf16[1024,1152]{1,0:T(8,128)(2,1)}), bf16[4096,1152]{1,0:T(8,128)(2,1)}) %all-gather.15.cloned.1.call-update) | async-done | bytes 9437200 | tf_op jit(solution)/shard_map/all_gather | solution.py:48
  1477.3 9.3 fusion.63
  1487.4 38.7 %reduce-scatter.20.cloned.1.call-done = f32[1024,288]{0,1:T(8,128)} async-done(((f32[4096,288]{0,1:T(8,128)}), f32[1024,288]{0,1:T(8,128)}) %reduce-scatter.20.cloned.1.call-update) | async-done | bytes 1179664 | tf_op jit(solution)/shard_map/reduce_scatter | solution.py:56
  1526.1 1.8 multiply_reduce_fusion.2
  1527.9 11.8 all-reduce.4
  1539.7 36.6 %reduce-scatter.16.cloned.1.call-done = f32[1024,288]{0,1:T(8,128)} async-done(((f32[4096,288]{0,1:T(8,128)}), f32[1024,288]{0,1:T(8,128)}) %reduce-scatter.16.cloned.1.call-update) | async-done | bytes 1179664 | tf_op jit(solution)/shard_map/reduce_scatter | solution.py:56
  1576.4 4.0 fusion.29
  1580.4 24.2 %all-gather.21.cloned.1.call-done = bf16[4096,288]{0,1:T(8,128)(2,1)} async-done(((bf16[1024,288]{0,1:T(8,128)(2,1)}), bf16[4096,288]{0,1:T(8,128)(2,1)}) %all-gather.21.cloned.1.call-update) | async-done | bytes 2359312 | tf_op jit(solution)/shard_map/all_gather | solution.py:30
  1604.6 5.2 fusion.71
  1610.1 85.1 %reduce-scatter.22.cloned.1.call-done = f32[1024,288]{0,1:T(8,128)} async-done(((f32[4096,288]{0,1:T(8,128)}), f32[1024,288]{0,1:T(8,128)}) %reduce-scatter.22.cloned.1.call-update) | async-done | bytes 1179664 | tf_op jit(solution)/shard_map/reduce_scatter | solution.py:37
  1695.2 1.3 convert_element_type.128
  1696.6 8.4 fusion.2
  1705.0 13.0 multiply_reduce_fusion
  1718.0 10.7 multiply_convert_fusion
  1728.8 6.4 convolution_multiply_fusion
  1735.2 2.7 convolution_multiply_fusion.1
  1737.9 2.8 fusion.58
  1740.7 128.8 %all-gather.23.cloned.1.call-done = bf16[4096,864]{0,1:T(8,128)(2,1)} async-done(((bf16[1024,864]{0,1:T(8,128)(2,1)}), bf16[4096,864]{0,1:T(8,128)(2,1)}) %all-gather.23.cloned.1.call-update) | async-done | bytes 7077904 | tf_op jit(solution)/shard_map/all_gather | solution.py:48
  1869.6 7.9 fusion.66
  1877.8 9.6 fusion.69
  1887.4 7.0 fusion.72
  1894.4 2.2 fusion.68
  1896.6 4.9 fusion.67
  1901.5 22.2 reduce-scatter.24.cloned.1.call-done
  1923.7 1.9 fusion.26
  1925.6 11.9 all-reduce.3
  1937.5 3.3 multiply_reduce_fusion.3
  1940.8 5.2 all_gather.35
  1946.1 2.8 fusion.32
  1950.0 1.8 fusion.35
  1951.8 14.1 all-reduce.1
  1966.0 1.9 slice_reduce_fusion.1
  1967.9 33.9 %all-reduce.2 = (f32[2,288]{1,0:T(2,128)}, f32[1152]{0:T(1024)}) all-reduce(f32[2,288]{1,0:T(2,128)S(1)} %pad_maximum_fusion.1, f32[1152]{0:T(1024)S(1)} %get-tuple-element.112), channel_id=1, replica_groups=mesh['dp'=2,'row'=4,'col'=4] {'dp','row'}, use_global_device_ids=true, to_apply=%region_41.42 | all-reduce | flops 1728 | bytes 13824 | tf_op jit(solution)/shard_map/psum | solution.py:276
  2001.9 9.1 psum.143
  2011.0 108.0 %all-reduce.11.cloned.1.call-done = (f32[288,6,288]{2,0,1:T(8,128)}, f32[288,3,288]{0,2,1:T(8,128)}, f32[288,288]{1,0:T(8,128)}, f32[288,1152]{1,0:T(8,128)}, f32[1152,288]{0,1:T(8,128)}) async-done(((f32[288,6,288]{2,0,1:T(8,128)}, f32[288,3,288]{0,2,1:T(8,128)}, f32[288,288]{1,0:T(8,128)}, f32[288,1152]{1,0:T(8,128)}, f32[1152,288]{0,1:T(8,128)}), (f32[288,6,288]{2,0,1:T(8,128)}, ...) | async-done | bytes 5971984 | tf_op jit(solution)/shard_map/psum | solution.py:273
  2118.9 2.9 copy.48
  2121.8 81.5 %all-reduce.9.cloned.1.call-done = f32[1000,288]{0,1:T(8,128)} async-done(((f32[1000,288]{0,1:T(8,128)}), f32[1000,288]{0,1:T(8,128)}) %all-reduce.9.cloned.1.call-update) | async-done | bytes 1152016 | tf_op jit(solution)/shard_map/psum | solution.py:276
  2203.3 2.4 copy.66
  2205.7 3.6 copy.67
  (159 shorter events, 20.6 us)
Async XLA Ops:
  7.2 27.5 %copy-start = (bf16[288,6,288]{2,0,1:T(8,128)(2,1)S(1)}, bf16[288,6,288]{2,0,1:T(8,128)(2,1)}, u32[]{:S(2)}) copy-start(bf16[288,6,288]{2,0,1:T(8,128)(2,1)} %param.19) | copy-start | bytes 2985988
  7.2 38.3 %copy-start.31 = (u32[32]{0:T(128)S(1)}, u32[32]{0:T(128)}, u32[]{:S(2)}) copy-start(u32[32]{0:T(128)} %constant.91) | copy-start | bytes 388
  7.2 39.6 %copy-start.2 = (bf16[1024,288]{0,1:T(8,128)(2,1)S(1)}, bf16[1024,288]{0,1:T(8,128)(2,1)}, u32[]{:S(2)}) copy-start(bf16[1024,288]{0,1:T(8,128)(2,1)} %param.15) | copy-start | bytes 1769476
  7.2 64.8 %all-gather.9.cloned.1.call-start = ((), (), s32[]{:S(2)}) async-start(), calls=%async_computation.8 | async-start | bytes 2949120 | tf_op jit(solution)/shard_map/all_gather | solution.py:30
  9.2 38.8 %copy-start.16 = (bf16[288,3,288]{2,0,1:T(8,128)(2,1)S(1)}, bf16[288,3,288]{2,0,1:T(8,128)(2,1)}, u32[]{:S(2)}) copy-start(bf16[288,3,288]{2,0,1:T(8,128)(2,1)} %param.21) | copy-start | bytes 1492996
  22.9 25.1 %copy-start.18 = (f32[1,1024]{1,0:T(1,128)}, f32[1,1024]{1,0:T(1,128)S(1)}, u32[]{:S(2)}) copy-start(f32[1,1024]{1,0:T(1,128)S(1)} %broadcast_multiply_fusion.3) | copy-start | bytes 12292
  32.5 15.4 copy-start.22
  34.7 13.2 copy-start.20
  46.8 1.1 copy-start.24
  48.0 270.2 %reduce-scatter.10.cloned.1.call-start = ((), (), s32[]{:S(2)}) async-start(), calls=%async_computation.9 | async-start | bytes 17694720 | tf_op jit(solution)/shard_map/reduce_scatter | solution.py:37
  48.4 32.3 %copy-start.7 = (bf16[288,3,288]{0,2,1:T(8,128)(2,1)}, bf16[288,3,288]{0,2,1:T(8,128)(2,1)S(1)}, u32[]{:S(2)}) copy-start(bf16[288,3,288]{0,2,1:T(8,128)(2,1)S(1)} %copy.40) | copy-start | bytes 1492996
  80.7 0.7 copy-start.26
  80.8 316.5 %all-gather.11.cloned.1.call-start = ((), (), s32[]{:S(2)}) async-start(), calls=%async_computation.10 | async-start | bytes 2949120 | tf_op jit(solution)/shard_map/all_gather | solution.py:48
  320.4 16.7 copy-start.3
  337.2 60.2 %copy-start.15 = (bf16[288,288]{1,0:T(8,128)(2,1)S(1)}, bf16[288,288]{1,0:T(8,128)(2,1)}, u32[]{:S(2)}) copy-start(bf16[288,288]{1,0:T(8,128)(2,1)} %param.23) | copy-start | bytes 497668
  345.7 103.7 %reduce-scatter.12.cloned.1.call-start = ((), (), s32[]{:S(2)}) async-start(), calls=%async_computation.11 | async-start | bytes 5898240 | tf_op jit(solution)/shard_map/reduce_scatter | solution.py:56
  402.5 1.1 copy-start.11
  402.5 2.2 copy-start.29
  402.6 73.0 %all-gather.17.cloned.1.call-start = ((), (), s32[]{:S(2)}) async-start(), calls=%async_computation.16 | async-start | bytes 2949120 | tf_op jit(solution)/shard_map/all_gather | solution.py:30
  404.6 97.1 %all-gather.13.cloned.1.call-start = ((), (), s32[]{:S(2)}) async-start(), calls=%async_computation.12 | async-start | bytes 2949120 | tf_op jit(solution)/shard_map/all_gather | solution.py:30
  472.3 345.8 %reduce-scatter.18.cloned.1.call-start = ((), (), s32[]{:S(2)}) async-start(), calls=%async_computation.17 | async-start | bytes 23592960 | tf_op jit(solution)/shard_map/reduce_scatter | solution.py:37
  486.6 648.7 %reduce-scatter.14.cloned.1.call-start = ((), (), s32[]{:S(2)}) async-start(), calls=%async_computation.13 | async-start | bytes 23592960 | tf_op jit(solution)/shard_map/reduce_scatter | solution.py:37
  512.8 0.7 copy-start.27
  512.9 798.0 %all-gather.19.cloned.1.call-start = ((), (), s32[]{:S(2)}) async-start(), calls=%async_computation.18 | async-start | bytes 11796480 | tf_op jit(solution)/shard_map/all_gather | solution.py:48
  1142.8 334.5 %all-gather.15.cloned.1.call-start = ((), (), s32[]{:S(2)}) async-start(), calls=%async_computation.14 | async-start | bytes 11796480 | tf_op jit(solution)/shard_map/all_gather | solution.py:48
  1143.4 382.7 %reduce-scatter.20.cloned.1.call-start = ((), (), s32[]{:S(2)}) async-start(), calls=%async_computation.19 | async-start | bytes 5898240 | tf_op jit(solution)/shard_map/reduce_scatter | solution.py:56
  1320.2 256.1 %reduce-scatter.16.cloned.1.call-start = ((), (), s32[]{:S(2)}) async-start(), calls=%async_computation.15 | async-start | bytes 5898240 | tf_op jit(solution)/shard_map/reduce_scatter | solution.py:56
  1486.7 0.7 copy-start.30
  1486.7 117.9 %all-gather.21.cloned.1.call-start = ((), (), s32[]{:S(2)}) async-start(), calls=%async_computation.20 | async-start | bytes 2949120 | tf_op jit(solution)/shard_map/all_gather | solution.py:30
  1580.4 114.9 %reduce-scatter.22.cloned.1.call-start = ((), (), s32[]{:S(2)}) async-start(), calls=%async_computation.21 | async-start | bytes 5898240 | tf_op jit(solution)/shard_map/reduce_scatter | solution.py:37
  1609.8 259.8 %all-gather.23.cloned.1.call-start = ((), (), s32[]{:S(2)}) async-start(), calls=%async_computation.22 | async-start | bytes 8847360 | tf_op jit(solution)/shard_map/all_gather | solution.py:48
  1696.6 21.4 slice-start
  1696.6 21.4 slice-start.1
  1705.0 13.0 slice-start.2
  1705.0 13.1 slice-start.3
  1728.8 6.4 copy-start.1
  1735.2 2.7 copy-start.10
  1737.9 131.7 %copy-start.8 = (bf16[288,3,288]{0,2,1:T(8,128)(2,1)S(1)}, bf16[288,3,288]{0,2,1:T(8,128)(2,1)}, u32[]{:S(2)}) copy-start(bf16[288,3,288]{0,2,1:T(8,128)(2,1)} %copy-done.7) | copy-start | bytes 1492996
  1740.7 183.0 %reduce-scatter.24.cloned.1.call-start = ((), (), s32[]{:S(2)}) async-start(), calls=%async_computation.23 | async-start | bytes 5898240 | tf_op jit(solution)/shard_map/reduce_scatter | solution.py:56
  1877.5 241.4 %all-reduce.11.cloned.1.call-start = ((), (), s32[]{:S(2)}) async-start(), calls=%async_computation.25 | async-start | bytes 14155776 | tf_op jit(solution)/shard_map/psum | solution.py:273
  1877.8 9.6 copy-start.5
  1877.8 18.8 slice-start.4
  1887.4 7.0 copy-start.6
  1887.4 7.0 copy-start.12
  1887.4 9.2 slice-start.5
  1894.4 2.2 copy-start.9
  1896.6 27.1 %copy-start.19 = (f32[1,1024]{1,0:T(1,128)S(1)}, f32[1,1024]{1,0:T(1,128)}, u32[]{:S(2)}) copy-start(f32[1,1024]{1,0:T(1,128)} %copy-done.18) | copy-start | bytes 12292
  1896.6 27.1 %copy-start.23 = (f32[1,1024]{1,0:T(1,128)S(1)}, f32[1,1024]{1,0:T(1,128)}, u32[]{:S(2)}) copy-start(f32[1,1024]{1,0:T(1,128)} %copy-done.22) | copy-start | bytes 12292
  1896.6 27.1 %copy-start.25 = (f32[288]{0:T(512)S(1)}, f32[288]{0:T(512)}, u32[]{:S(2)}) copy-start(f32[288]{0:T(512)} %copy-done.24) | copy-start | bytes 3460
  1923.7 13.9 copy-start.4
  1937.5 8.5 copy-start.21
  1948.9 1.2 copy-start.28
  1948.9 254.4 %all-reduce.9.cloned.1.call-start = ((), (), s32[]{:S(2)}) async-start(), calls=%async_computation.24 | async-start | bytes 2359296 | tf_op jit(solution)/shard_map/psum | solution.py:276
  2205.7 3.6 copy-start.17
  2205.7 4.3 copy-start.14
  2209.3 1.8 copy-start.13
Sparse Core Ops, SparseCore 0:
  48.1 23.9 all-gather.8
  80.9 237.2 reduce-scatter.9
  345.8 51.4 all-gather.10
  402.7 46.6 reduce-scatter.11
  451.5 24.0 all-gather.16
  477.6 24.0 all-gather.12
  504.2 313.7 reduce-scatter.17
  820.4 314.8 reduce-scatter.13
  1143.0 167.8 all-gather.18
  1312.3 164.9 all-gather.14
  1480.0 46.0 reduce-scatter.19
  1528.5 47.8 reduce-scatter.15
  1580.5 24.0 all-gather.20
  1609.9 85.2 reduce-scatter.21
  1740.8 128.7 all-gather.22
  1877.6 46.0 reduce-scatter.23
  1949.0 169.8 all-reduce.10
  2123.3 80.0 all-reduce.8
where the time goes:
time: 2230 us; the launch traced here: 2220 us
  waiting for transfers between devices  1850 us (83%)
  matrix products  146 us (7%)
  blocking collectives  139 us (6%)
  other arithmetic  55.7 us (2%)
    reduce_scatter x4, waiting for transfers between devices, through_rows(): lax.psum_scatter(partial_term(jnp.int32(0), share * lax.axis_size('row'))...  943 us
    all_gather x4, waiting for transfers between devices, through_cols(): gathered = lax.all_gather(source, 'row', axis=0, tiled=True)  504 us
    reduce_scatter x4, waiting for transfers between devices, through_cols(): lax.psum_scatter(partial_term(jnp.int32(0), share * lax.axis_size('col'))...  142 us
    psum x1, waiting for transfers between devices, per_device(): lax.psum((d_w_qkv, d_w_out, d_w_fc1, d_w_fc2, d_ada_weight, d_ada_bias),...  108 us
    psum x1, waiting for transfers between devices, per_device(): lax.psum((d_table, d_query_value_bias, d_fc1_bias), ('dp', 'row'))  81.5 us
    dot_general x8, matrix products, contract_with(): lax.dot_general(left, weight, (((1,), (contract,)), ((), ())), preferred_...  67.8 us
    all_gather x4, waiting for transfers between devices, through_rows(): gathered = lax.all_gather(source, 'col', axis=0, tiled=True)  66.1 us
    psum x6, blocking collectives, feature_sums(): return lax.psum(parts, 'row')  65.8 us
  transfers between devices with their start and end apart: 18, of which 18 were waited for; matrix products, arithmetic and copies ran while one was open for 4% of the time, Pallas kernels for 0%

commit v1 on v0

v1 whole, which is shorter than its diff:
```python
from functools import partial
import math

import jax
import jax.numpy as jnp
from jax import lax
from jax.sharding import PartitionSpec as P

D = 1152
HD = 72
NCLS = 1000
SEQ = 1024


def time_embedding(time_ids):
    half_width = D // 2
    freqs = jnp.exp(-math.log(10000.0) * jnp.arange(half_width, dtype=jnp.float32) / half_width)
    angles = time_ids.astype(jnp.float32)[:, None] * freqs[None, :]
    return jnp.concatenate([jnp.cos(angles), jnp.sin(angles)], axis=-1)


def matmul(left, right, left_dim=1, right_dim=0):
    return lax.dot_general(
        left, right, (((left_dim,), (right_dim,)), ((), ())), preferred_element_type=jnp.float32
    )


def transposed(value):
    side = lax.axis_size("col")
    pairs = [(i * side + j, j * side + i) for i in range(side) for j in range(side)]
    return lax.ppermute(value, ("row", "col"), pairs)


def side_by_side(pieces):
    return jnp.concatenate([pieces[i] for i in range(pieces.shape[0])], axis=-1)


def gather_wide(value, axis_name):
    return side_by_side(lax.all_gather(value, axis_name, axis=0))


def in_blocks(wide, count):
    return jnp.stack(jnp.split(wide, count, axis=-1), axis=0)


def sum_scatter(blocks, axis_name):
    return lax.psum_scatter(
        blocks.astype(jnp.bfloat16), axis_name, scatter_dimension=0, tiled=False
    ).astype(jnp.float32)


def grad_sum(blocks):
    piece = lax.psum_scatter(
        blocks.astype(jnp.bfloat16), "row", scatter_dimension=0, tiled=False
    )
    both = lax.all_gather(piece, "dp", axis=0).astype(jnp.float32)
    return jnp.sum(both, axis=0)


def moments(values):
    mean = jnp.mean(values, axis=-1, keepdims=True)
    centred = values - mean
    spread = jnp.mean(centred * centred, axis=-1, keepdims=True)
    return mean, lax.rsqrt(spread + 1e-06)


def attend(queries, keys, values):
    scores = jnp.einsum("qhe,khe->hqk", queries, keys, preferred_element_type=jnp.float32) * (
        1.0 / math.sqrt(HD)
    )
    biggest = jnp.max(scores, axis=-1, keepdims=True)
    expo = jnp.exp(scores - biggest)
    totals = jnp.sum(expo, axis=-1, keepdims=True)
    weights = (expo / totals).astype(jnp.bfloat16)
    result = jnp.einsum("hqk,khe->qhe", weights, values, preferred_element_type=jnp.float32)
    return (result.reshape(SEQ, -1), (biggest + jnp.log(totals))[..., 0])


def attend_back(queries, keys, values, log_totals, d_result):
    scale = 1.0 / math.sqrt(HD)
    scores = jnp.einsum("qhe,khe->hqk", queries, keys, preferred_element_type=jnp.float32) * scale
    probs = jnp.exp(scores - log_totals[..., None])
    d_values = jnp.einsum(
        "hqk,qhe->khe", probs.astype(jnp.bfloat16), d_result, preferred_element_type=jnp.float32
    )
    d_probs = jnp.einsum("qhe,khe->hqk", d_result, values, preferred_element_type=jnp.float32)
    inner = jnp.sum(probs * d_probs, axis=-1, keepdims=True)
    d_scores = (probs * (d_probs - inner)).astype(jnp.bfloat16)
    d_queries = (
        jnp.einsum("hqk,khe->qhe", d_scores, keys, preferred_element_type=jnp.float32) * scale
    )
    d_keys = (
        jnp.einsum("hqk,qhe->khe", d_scores, queries, preferred_element_type=jnp.float32) * scale
    )
    return jnp.concatenate(
        [d_queries.reshape(SEQ, -1), d_keys.reshape(SEQ, -1), d_values.reshape(SEQ, -1)], axis=1
    ).astype(jnp.bfloat16)


def norm_back(d_input, scale_row, normed, inv_std, sums):
    d_normed = d_input * (1.0 + scale_row)
    return inv_std * (d_normed - sums[0][:, None] / D - normed * sums[1][:, None] / D)


def norm_sums(partial_input, scale_row, normed):
    d_normed = partial_input * (1.0 + scale_row)
    return lax.psum(
        jnp.stack([jnp.sum(d_normed, axis=-1), jnp.sum(d_normed * normed, axis=-1)]), "col"
    )


def per_device(
    tokens,
    class_ids,
    time_ids,
    class_table,
    adaptive_norm_weight,
    adaptive_norm_bias,
    query_key_value_weight,
    query_value_bias,
    w_out,
    out_bias,
    w_fc1,
    fc1_bias,
    w_fc2,
    fc2_bias,
    cotangent,
):
    highest = lax.Precision.HIGHEST
    f32 = jnp.float32
    bf16 = jnp.bfloat16
    rows, cols = lax.axis_size("row"), lax.axis_size("col")
    row, col = lax.axis_index("row"), lax.axis_index("col")
    width = class_table.shape[1]
    heads_here = width // HD
    local_lats = class_ids.shape[0]
    assert rows == cols == local_lats and tokens.shape[0] == SEQ

    tok_block = transposed(tokens)
    tok = gather_wide(tok_block, "col").astype(f32)
    tok_block = tok_block.astype(f32)
    dy_block = transposed(cotangent)
    dy = gather_wide(dy_block, "col").astype(f32)
    dy_block = dy_block.astype(f32)

    w_qkv = query_key_value_weight.reshape(width, 3 * width)
    w_qkv_all = lax.all_gather(w_qkv, "row", axis=0, tiled=True)
    w_out_here = gather_wide(w_out, "row")
    w_out_all = lax.all_gather(w_out_here, "col", axis=0, tiled=True)
    w_fc1_all = lax.all_gather(w_fc1, "row", axis=0, tiled=True)
    w_fc2_all = gather_wide(w_fc2, "row")

    def embed(labels, steps):
        onehot = (labels[:, None] == jnp.arange(NCLS, dtype=jnp.int32)[None, :]).astype(bf16)
        timing = lax.dynamic_slice_in_dim(time_embedding(steps), col * width, width, 1)
        return onehot, jnp.dot(onehot, class_table, preferred_element_type=f32) + timing

    here = jax.nn.silu(embed(class_ids, time_ids)[1]).astype(bf16)
    pieces = jnp.einsum("au,uop->aop", here, adaptive_norm_weight, preferred_element_type=f32)
    pieces = pieces + jnp.where(col == 0, 1.0, 0.0) * adaptive_norm_bias.astype(f32)[None]
    packed = jnp.concatenate(
        [
            pieces.reshape(local_lats * 6, width),
            out_bias.astype(f32)[None],
            fc2_bias.astype(f32)[None],
        ],
        axis=0,
    )
    packed = lax.all_gather(packed, ("row", "col"), axis=0).reshape(rows, cols, -1, width)
    mod_blocks = jnp.sum(
        lax.dynamic_slice_in_dim(packed, row * 6, 6, 2), axis=1
    )
    mod_here = lax.dynamic_index_in_dim(mod_blocks, col, 0, keepdims=False)
    mod = side_by_side(mod_blocks)
    bias_blocks = packed[:, 0, local_lats * 6 :]
    bias_here = lax.dynamic_index_in_dim(bias_blocks, col, 0, keepdims=False)
    out_bias_all = side_by_side(bias_blocks)[0]

    mean1, inv1 = moments(tok)
    normed1 = (tok - mean1) * inv1
    input1 = (normed1 * (1.0 + mod[1]) + mod[0]).astype(bf16)
    qv_bias = query_value_bias.astype(f32)
    qkv_bias = jnp.concatenate([qv_bias[0], jnp.zeros_like(qv_bias[0]), qv_bias[1]])
    qkv = (matmul(input1, w_qkv_all) + qkv_bias).astype(bf16)
    split = qkv.reshape(SEQ, 3, heads_here, HD)
    queries, keys, values = (split[:, 0], split[:, 1], split[:, 2])
    attended, log_totals = attend(queries, keys, values)
    attended = attended.astype(bf16)
    attended_all = gather_wide(attended, "col")
    branch = matmul(attended_all, w_out_all) + out_bias_all
    middle = tok + mod[2] * branch
    mean2, inv2 = moments(middle)
    normed2 = (middle - mean2) * inv2
    input2 = (normed2 * (1.0 + mod[4]) + mod[3]).astype(bf16)
    branch_here = lax.dynamic_slice_in_dim(branch, col * width, width, 1)
    middle_here = tok_block + mod_here[2] * branch_here
    normed2_here = (middle_here - mean2) * inv2
    normed1_here = (tok_block - mean1) * inv1

    hidden = matmul(input2, w_fc1_all) + fc1_bias.astype(f32)
    gelu_fn = partial(jax.nn.gelu, approximate=True)
    activ = gelu_fn(hidden).astype(bf16)
    feed = sum_scatter(in_blocks(matmul(activ, w_fc2_all), cols), "col") + bias_here[1]
    mixed = transposed((middle_here + mod_here[5] * feed).astype(bf16))

    d_feed = (dy * mod[5]).astype(bf16)
    d_hidden = jax.vjp(gelu_fn, hidden)[1](matmul(d_feed, w_fc2_all, 1, 1))[0].astype(bf16)
    d_input2 = matmul(d_hidden, w_fc1_all, 1, 1)
    sums2 = norm_sums(d_input2, mod[4], normed2)
    d_input2 = sum_scatter(in_blocks(d_input2, cols), "col")
    d_w_fc2 = grad_sum(in_blocks(matmul(activ, d_feed, 0, 0), rows))
    d_w_fc1 = grad_sum(matmul(input2, d_hidden, 0, 0).reshape(rows, width, -1))
    d_fc1_bias = jnp.sum(d_hidden.astype(f32), axis=0)
    d_fc2_bias = jnp.sum((dy_block * mod_here[5]).astype(bf16).astype(f32), axis=0)
    d_middle = dy_block + norm_back(d_input2, mod_here[4], normed2_here, inv2, sums2)
    d_branch_here = (d_middle * mod_here[2]).astype(bf16)
    d_branch = gather_wide(d_branch_here, "col")
    d_attended = matmul(d_branch, w_out_here, 1, 1).astype(bf16).reshape(SEQ, heads_here, HD)
    d_w_out = grad_sum(in_blocks(matmul(attended, d_branch, 0, 0), rows))
    d_out_bias = jnp.sum(d_branch_here.astype(f32), axis=0)

    early = jnp.stack(
        [
            jnp.sum(d_middle * branch_here, axis=0),
            jnp.sum(d_input2, axis=0),
            jnp.sum(d_input2 * normed2_here, axis=0),
            jnp.sum(dy_block * feed, axis=0),
            d_out_bias,
            d_fc2_bias,
        ]
    )

    d_qkv = attend_back(queries, keys, values, log_totals, d_attended)
    d_input1 = matmul(d_qkv, w_qkv_all, 1, 1)
    sums1 = norm_sums(d_input1, mod[1], normed1)
    d_input1 = sum_scatter(in_blocks(d_input1, cols), "col")
    d_w_qkv = grad_sum(matmul(input1, d_qkv, 0, 0).reshape(rows, width, 3 * width))
    d_w_qkv = d_w_qkv.reshape(width, 3, width)
    d_qkv_sums = jnp.sum(d_qkv.astype(f32), axis=0).reshape(3, width)
    d_tokens = d_middle + norm_back(d_input1, mod_here[1], normed1_here, inv1, sums1)
    d_tokens = transposed(d_tokens.astype(bf16)).astype(f32)

    late = jnp.stack([jnp.sum(d_input1, axis=0), jnp.sum(d_input1 * normed1_here, axis=0)])

    def every_latent(part):
        full = lax.all_gather(part, ("dp", "row", "col"), axis=0)
        full = full.reshape(-1, cols, part.shape[0], width)
        return lax.dynamic_index_in_dim(full, row, 1, keepdims=False)

    early, late = every_latent(early), every_latent(late)
    d_out_bias = jnp.sum(early[:, 4], axis=0)
    d_fc2_bias = jnp.sum(early[:, 5], axis=0)
    d_mod = jnp.concatenate([late, early[:, :4]], axis=1)
    d_ada_bias = jnp.sum(d_mod, axis=0)
    all_ids = lax.all_gather(jnp.stack([class_ids, time_ids]), "dp", axis=1, tiled=True)
    onehot, condition = embed(all_ids[0], all_ids[1])
    activated = jax.nn.silu(condition).astype(bf16).astype(f32)
    d_ada_weight = jnp.einsum("qk,qfb->kfb", activated, d_mod, precision=highest)
    d_activated = jnp.einsum(
        "qnp,unp->qu", d_mod, adaptive_norm_weight.astype(f32), precision=highest
    )
    d_activated = lax.psum(d_activated, "row")
    d_condition = jax.vjp(jax.nn.silu, condition)[1](d_activated)[0]
    d_table = lax.dot_general(
        onehot.astype(f32), d_condition, (((0,), (0,)), ((), ())), precision=highest
    )
    bias_sums = lax.psum(
        jnp.concatenate([d_fc1_bias, d_qkv_sums[0], d_qkv_sums[2]]), ("dp", "row")
    )
    d_fc1_bias = bias_sums[: d_fc1_bias.shape[0]]
    d_query_value_bias = bias_sums[d_fc1_bias.shape[0] :].reshape(2, width)
    return (
        mixed,
        d_tokens,
        d_table,
        d_ada_weight,
        d_ada_bias,
        d_w_qkv,
        d_query_value_bias,
        d_w_out,
        d_out_bias,
        d_w_fc1,
        d_fc1_bias,
        d_w_fc2,
        d_fc2_bias,
    )


def solution(mesh):
    return jax.shard_map(
        per_device,
        mesh=mesh,
        in_specs=(
            P(("dp", "col"), "row"),
            P("dp"),
            P("dp"),
            P(None, "col"),
            P("col", None, "row"),
            P(None, "row"),
            P("row", None, "col"),
            P(None, "col"),
            P("col", "row"),
            P("row"),
            P("row", "col"),
            P("col"),
            P("col", "row"),
            P("row"),
            P(("dp", "col"), "row"),
        ),
        out_specs=(
            P(("dp", "col"), "row"),
            P(("dp", "col"), "row"),
            P(None, "col"),
            P("col", None, "row"),
            P(None, "row"),
            P("row", None, "col"),
            P(None, "col"),
            P("col", "row"),
            P("row"),
            P("row", "col"),
            P("col"),
            P("col", "row"),
            P("row"),
        ),
        check_vma=False,
    )
```

time: 2230 us -> 911 us (0.41)
  waiting for transfers between devices: 1850 us -> 363 us
  blocking collectives: 139 us -> 288 us
  local copies, waits for them, and re-layouts: 15.8 us -> 59.7 us
  matrix products: 146 us -> 114 us
    reduce_scatter x8 -> x7, waiting for transfers between devices: 1090 us -> 167 us  [the longest x4 106 us: grad_sum(): lax.psum_scatter(blocks.astype(jnp.bfloat16), 'row', scatter_dimension=0,...]
    all_gather x8 -> x10, waiting for transfers between devices: 570 us -> 195 us  [the longest x5 81 us: gather_wide(): return side_by_side(lax.all_gather(value, axis_name, axis=0))]
    psum x2 -> x0, waiting for transfers between devices: 189 us -> none  [the longest x1 108 us: per_device(): lax.psum((d_w_qkv, d_w_out, d_w_fc1, d_w_fc2, d_ada_weight, d_ada_bias),...]
    all_gather x1 -> x7, blocking collectives: 5.23 us -> 193 us  [the longest x2 78.5 us: every_latent(): full = lax.all_gather(part, ('dp', 'row', 'col'), axis=0)]
    psum x9 -> x4, blocking collectives: 123 us -> 94.9 us  [the longest x1 57.6 us: per_device(): d_activated = lax.psum(d_activated, 'row')]
    dot_general x17, matrix products: 98.7 us -> 74 us  [the longest x12 66.2 us: matmul(): lax.dot_general(left, right, (((left_dim,), (right_dim,)), ((), ())), pre...]
  transfers between devices with their start and end apart: 18 -> 21, of which waited for: 18 -> 13; matrix products, arithmetic and copies ran while one was open for 4% -> 22% of each run, Pallas kernels for 0% -> 0%
where the time goes in v1:
time: 911 us; the launch traced here: 910 us
  waiting for transfers between devices  363 us (40%)
  blocking collectives  288 us (32%)
  matrix products  114 us (13%)
  other arithmetic  63.1 us (7%)
  local copies, waits for them, and re-layouts  59.7 us (7%)
  between operations  15.2 us (2%)
    reduce_scatter x4, waiting for transfers between devices, grad_sum(): lax.psum_scatter(blocks.astype(jnp.bfloat16), 'row', scatter_dimension=0,...  106 us
    all_gather x5, waiting for transfers between devices, gather_wide(): return side_by_side(lax.all_gather(value, axis_name, axis=0))  81 us
    all_gather x2, blocking collectives, every_latent(): full = lax.all_gather(part, ('dp', 'row', 'col'), axis=0)  78.5 us
    dot_general x12, matrix products, matmul(): lax.dot_general(left, right, (((left_dim,), (right_dim,)), ((), ())), pre...  66.2 us
    reduce_scatter x3, waiting for transfers between devices, sum_scatter(): lax.psum_scatter(blocks.astype(jnp.bfloat16), axis_name, scatter_dimensio...  60.8 us
    psum x1, blocking collectives, per_device(): d_activated = lax.psum(d_activated, 'row')  57.6 us
    all_gather x1, blocking collectives, per_device(): lax.all_gather(packed, ('row', 'col'), axis=0)  56 us
    all_gather x1, waiting for transfers between devices, per_device(): w_fc1_all = lax.all_gather(w_fc1, 'row', axis=0, tiled=True)  44.6 us
  transfers between devices with their start and end apart: 21, of which 13 were waited for; matrix products, arithmetic and copies ran while one was open for 22% of the time, Pallas kernels for 0%

profile of v1, /device:TPU:0, one launch (start us, length us, event | category | flops | bytes accessed | tf_op | source)
XLA Modules:
  0.0 910.0 jit_solution(1250965841579221006)
XLA Ops:
  17.0 56.0 %all-gather.8 = f32[16,26,288]{2,1,0:T(8,128)S(1)} all-gather(f32[1,26,288]{2,1,0:T(8,128)S(1)} %maximum_bitcast_fusion), channel_id=2, replica_groups=mesh['dp'=2,'row'=4,'col'=4] {'row','col'}, dimensions={0}, use_global_device_ids=true | all-gather | bytes 509184 | tf_op jit(solution)/shard_map/all_gather | solution.py:169
  75.6 3.7 all-gather.35.cloned.1.call-done
  79.3 3.3 fusion.102
  82.6 5.3 concatenate.48
  87.9 2.2 convert_reduce_fusion
  91.1 44.5 %all-gather.23.cloned.1.call-done = bf16[1152,864]{1,0:T(8,128)(2,1)} async-done(((bf16[288,864]{1,0:T(8,128)(2,1)}), bf16[1152,864]{1,0:T(8,128)(2,1)}) %all-gather.23.cloned.1.call-update) | async-done | bytes 1990672 | tf_op jit(solution)/shard_map/all_gather | solution.py:147
  135.6 5.1 add_convert_fusion.1
  140.7 8.2 multiply_reduce_fusion.1
  149.0 8.6 fusion
  157.6 8.5 fusion.54
  166.2 33.6 %all-gather.2 = bf16[1152,288]{1,0:T(8,128)(2,1)S(1)} all-gather(bf16[288,288]{1,0:T(8,128)(2,1)S(1)} %copy-done.31), channel_id=4, replica_groups=mesh['dp'=2,'row'=4,'col'=4] {'row'}, dimensions={0}, use_global_device_ids=true | all-gather | bytes 829440 | tf_op jit(solution)/shard_map/all_gather | solution.py:39
  202.9 2.4 all-gather.37.cloned.1.call-done
  205.3 2.7 fusion.103
  208.0 21.5 %all-gather.39.cloned.1.call-done = bf16[4096,288]{0,1:T(8,128)(2,1)} async-done(((bf16[1024,288]{0,1:T(8,128)(2,1)}), bf16[4096,288]{0,1:T(8,128)(2,1)}) %all-gather.39.cloned.1.call-update) | async-done | bytes 2359312 | tf_op jit(solution)/shard_map/all_gather | solution.py:39
  229.5 3.1 fusion.104
  232.6 23.0 %all-gather.25.cloned.1.call-done = bf16[4,1024,288]{1,2,0:T(8,128)(2,1)} async-done(((bf16[1,1024,288]{1,2,0:T(8,128)(2,1)}), bf16[4,1024,288]{1,2,0:T(8,128)(2,1)}) %all-gather.25.cloned.1.call-update) | async-done | bytes 2359312 | tf_op jit(solution)/shard_map/all_gather | solution.py:39
  255.6 3.1 slice_bitcast_fusion.19
  258.7 24.7 %all-gather.27.cloned.1.call-done = bf16[1152,1152]{1,0:T(8,128)(2,1)} async-done(((bf16[288,1152]{1,0:T(8,128)(2,1)}), bf16[1152,1152]{1,0:T(8,128)(2,1)}) %all-gather.27.cloned.1.call-update) | async-done | bytes 2654224 | tf_op jit(solution)/shard_map/all_gather | solution.py:149
  283.4 7.6 fusion.98
  293.2 2.5 add_convert_fusion
  295.7 44.6 %all-gather.29.cloned.1.call-done = bf16[1152,1152]{1,0:T(8,128)(2,1)} async-done(((bf16[288,1152]{1,0:T(8,128)(2,1)}), bf16[1152,1152]{1,0:T(8,128)(2,1)}) %all-gather.29.cloned.1.call-update) | async-done | bytes 2654224 | tf_op jit(solution)/shard_map/all_gather | solution.py:150
  340.4 6.1 convolution_add_fusion
  346.6 7.3 convert_reduce_fusion.1
  354.0 5.4 multiply_reduce_fusion.5
  360.6 2.1 pad_maximum_fusion.1
  364.1 6.0 convolution_convert_fusion
  370.4 2.0 pad_maximum_fusion.4
  372.4 7.2 convolution_convert_fusion.1
  381.5 7.4 psum.28
  389.0 10.9 %reduce-scatter.10.cloned.1.call-done = bf16[1,1024,288]{2,1,0:T(8,128)(2,1)} async-done(((bf16[4,1024,288]{2,1,0:T(8,128)(2,1)}), bf16[1,1024,288]{2,1,0:T(8,128)(2,1)}) %reduce-scatter.10.cloned.1.call-update) | async-done | bytes 589840 | tf_op jit(solution)/shard_map/reduce_scatter | solution.py:47
  399.9 4.3 convert_reduce_fusion.9
  404.3 50.7 %reduce-scatter.20.cloned.1.call-done = bf16[1,1152,288]{1,2,0:T(8,128)(2,1)} async-done(((bf16[4,1152,288]{1,2,0:T(8,128)(2,1)}), bf16[1,1152,288]{1,2,0:T(8,128)(2,1)}) %reduce-scatter.20.cloned.1.call-update) | async-done | bytes 663568 | tf_op jit(solution)/shard_map/reduce_scatter | solution.py:53
  455.1 55.1 %reduce-scatter.18.cloned.1.call-done = bf16[1,288,1152]{2,1,0:T(8,128)(2,1)} async-done(((bf16[4,288,1152]{2,1,0:T(8,128)(2,1)}), bf16[1,288,1152]{2,1,0:T(8,128)(2,1)}) %reduce-scatter.18.cloned.1.call-update) | async-done | bytes 663568 | tf_op jit(solution)/shard_map/reduce_scatter | solution.py:53
  510.2 30.4 %all-gather.41.cloned.1.call-done = bf16[4096,288]{1,0:T(8,128)(2,1)} async-done(((bf16[1024,288]{1,0:T(8,128)(2,1)}), bf16[4096,288]{1,0:T(8,128)(2,1)}) %all-gather.41.cloned.1.call-update) | async-done | bytes 2359312 | tf_op jit(solution)/shard_map/all_gather | solution.py:39
  540.6 3.3 fusion.101
  543.9 5.6 concatenate.56
  549.5 3.1 convolution_convert_fusion.5
  553.6 7.4 fusion.51
  562.5 11.5 %multiply_reduce_fusion = (f32[4,1024]{1,0:T(4,128)S(1)}, f32[4,1024,1024]{1,2,0:T(8,128)}) fusion(f32[4,1024,1024]{1,2,0:T(8,128)} %get-tuple-element.149, f32[4,1024]{1,0:T(4,128)S(1)} %log_add_fusion, bf16[1024,4,72]{0,2,1:T(8,128)(2,1)S(1)} %bitcast.223, bf16[1024,3,4,72]{0,3,2,1:T(8,128)(2,1)} %bitcast.207), kind=kOutput, calls=%fused_computation.1 | convolution fusion | flops 620752896 | bytes 34766848 | tf_op jit(solution)/shard_map/qhe,khe->hqk/dot_general | solution.py:86
  574.0 12.9 %multiply_convert_fusion = bf16[4,1024,1024]{1,2,0:T(8,128)(2,1)S(1)} fusion(f32[4,1024,1024]{1,2,0:T(8,128)} %get-tuple-element.154, f32[4,1024,1024]{1,2,0:T(8,128)} %get-tuple-element.149, f32[4,1024]{1,0:T(4,128)S(1)} %get-tuple-element.153, f32[4,1024]{1,0:T(4,128)S(1)} %log_add_fusion), kind=kLoop, calls=%fused_computation | loop fusion | flops 20971520 | bytes 41975808 | tf_op jit(solution)/shard_map/convert_element_type | solution.py:88
  587.0 2.7 fusion.50
  592.1 3.9 convolution_convert_fusion.3
  596.1 4.1 copy.66
  600.2 6.3 multiply_reduce_fusion.4
  607.9 2.3 pad_maximum_fusion.2
  611.2 7.1 convolution_convert_fusion.2
  619.6 2.1 pad_maximum_fusion
  622.4 4.2 all-gather.9
  629.4 2.7 convert_reduce_fusion.3
  632.1 2.7 convert_reduce_fusion.4
  636.5 23.7 %psum.31 = f32[1728]{0:T(1024)S(1)} all-reduce(f32[1728]{0:T(1024)S(1)} %concatenate.60), channel_id=1, replica_groups=mesh['dp'=2,'row'=4,'col'=4] {'dp','row'}, use_global_device_ids=true, to_apply=%region_31.32 | all-reduce | flops 1728 | bytes 13824 | tf_op jit(solution)/shard_map/psum | solution.py:267
  660.9 6.2 psum.29
  667.2 7.6 all_gather.98
  675.6 13.0 %all_gather.97 = bf16[2,288,864]{2,1,0:T(8,128)(2,1)S(1)} all-gather(bf16[1,288,864]{2,1,0:T(8,128)(2,1)} %reduce-scatter.14.cloned.1.call-done), channel_id=1, replica_groups=mesh['dp'=2,'row'=4,'col'=4] {'dp'}, dimensions={0}, use_global_device_ids=true | all-gather | bytes 1492992 | tf_op jit(solution)/shard_map/all_gather | solution.py:56
  689.8 2.7 copy.67
  692.5 2.9 copy.68
  695.4 10.7 %reduce-scatter.12.cloned.1.call-done = bf16[1,1024,288]{2,1,0:T(8,128)(2,1)} async-done(((bf16[4,1024,288]{2,1,0:T(8,128)(2,1)}), bf16[1,1024,288]{2,1,0:T(8,128)(2,1)}) %reduce-scatter.12.cloned.1.call-update) | async-done | bytes 589840 | tf_op jit(solution)/shard_map/reduce_scatter | solution.py:47
  707.4 39.2 %reduce-scatter.8.cloned.1.call-done = bf16[1,1024,288]{2,1,0:T(8,128)(2,1)} async-done(((bf16[4,1024,288]{2,1,0:T(8,128)(2,1)}), bf16[1,1024,288]{2,1,0:T(8,128)(2,1)}) %reduce-scatter.8.cloned.1.call-update) | async-done | bytes 589840 | tf_op jit(solution)/shard_map/reduce_scatter | solution.py:47
  746.7 5.3 fusion.41
  752.0 40.8 %all-gather.10 = f32[32,2,288]{2,1,0:T(2,128)S(1)} all-gather(f32[1,2,288]{2,1,0:T(2,128)S(1)} %maximum_bitcast_fusion.1), channel_id=8, replica_groups=mesh['dp'=2,'row'=4,'col'=4] {'dp','row','col'}, dimensions={0}, use_global_device_ids=true | all-gather | bytes 76032 | tf_op jit(solution)/shard_map/all_gather | solution.py:246
  792.8 37.7 %all-gather.11 = f32[32,6,288]{2,1,0:T(8,128)S(1)} all-gather(f32[1,6,288]{2,1,0:T(8,128)S(1)} %bitcast.236), channel_id=9, replica_groups=mesh['dp'=2,'row'=4,'col'=4] {'dp','row','col'}, dimensions={0}, use_global_device_ids=true | all-gather | bytes 228096 | tf_op jit(solution)/shard_map/all_gather | solution.py:246
  832.0 2.2 copy.62
  839.2 57.6 %psum.30 = f32[8,288]{1,0:T(8,128)S(1)} all-reduce(f32[8,288]{1,0:T(8,128)S(1)} %convolution_bitcast_fusion), channel_id=1, replica_groups=mesh['dp'=2,'row'=4,'col'=4] {'row'}, use_global_device_ids=true, to_apply=%region_25.26 | all-reduce | flops 2304 | bytes 18432 | tf_op jit(solution)/shard_map/psum | solution.py:262
  898.5 2.8 fusion.59
  (278 shorter events, 51.2 us)
Async XLA Ops:
  7.2 8.9 copy-start
  7.2 8.2 copy-start.65
  7.2 8.2 copy-start.63
  7.2 8.2 copy-start.64
  7.2 8.3 copy-start.57
  7.2 8.9 copy-start.13
  7.2 8.8 copy-start.60
  7.3 72.1 %all-gather.35.cloned.1.call-start = ((), (), s32[]{:S(2)}) async-start(), calls=%async_computation.20 | async-start | bytes 3932160 | tf_op jit(solution)/shard_map/all_gather | solution.py:39
  7.3 1.9 collective-permute-start
  10.3 62.6 %copy-start.62 = (bf16[2,288]{1,0:T(2,128)(2,1)S(1)}, bf16[2,288]{1,0:T(2,128)(2,1)}, u32[]{:S(2)}) copy-start(bf16[2,288]{1,0:T(2,128)(2,1)} %param.22) | copy-start | bytes 3460
  10.4 125.2 %all-gather.23.cloned.1.call-start = ((), (), s32[]{:S(2)}) async-start(), calls=%async_computation.7 | async-start | bytes 2580480 | tf_op jit(solution)/shard_map/all_gather | solution.py:147
  12.9 192.3 %all-gather.37.cloned.1.call-start = ((), (), s32[]{:S(2)}) async-start(), calls=%async_computation.21 | async-start | bytes 3317760 | tf_op jit(solution)/shard_map/all_gather | solution.py:39
  13.7 215.9 %all-gather.39.cloned.1.call-start = ((), (), s32[]{:S(2)}) async-start(), calls=%async_computation.22 | async-start | bytes 2949120 | tf_op jit(solution)/shard_map/all_gather | solution.py:39
  13.7 60.8 %collective-permute-start.2 = (bf16[1024,288]{0,1:T(8,128)(2,1)}, bf16[1024,288]{0,1:T(8,128)(2,1)S(1)}, u32[]{:S(2)}, u32[]{:S(2)}) collective-permute-start(bf16[1024,288]{0,1:T(8,128)(2,1)} %param.29), channel_id=1, source_target_pairs={{0,0},{1,4},{2,8},{3,12},{4,1},{5,5},{6,9},{7,13},{8,2},{9,6},{10,... | collective-permute-start | bytes 1769480 | tf_op jit(solution)/shard_map/ppermute | solution.py:31
  74.5 66.2 %copy-start.49 = (f32[1152]{0:T(1024)}, f32[1152]{0:T(1024)S(1)}, u32[]{:S(2)}) copy-start(f32[1152]{0:T(1024)S(1)} %get-tuple-element.72) | copy-start | bytes 13828
  74.5 66.2 %copy-start.51 = (f32[1152]{0:T(1024)}, f32[1152]{0:T(1024)S(1)}, u32[]{:S(2)}) copy-start(f32[1152]{0:T(1024)S(1)} %get-tuple-element.71) | copy-start | bytes 13828
  75.4 180.2 %all-gather.25.cloned.1.call-start = ((), (), s32[]{:S(2)}) async-start(), calls=%async_computation.8 | async-start | bytes 2949120 | tf_op jit(solution)/shard_map/all_gather | solution.py:39
  87.9 47.6 %copy-start.59 = (f32[864]{0:T(1024)S(1)}, f32[864]{0:T(1024)}, u32[]{:S(2)}) copy-start(f32[864]{0:T(1024)} %pad_maximum_fusion.16) | copy-start | bytes 10372
  90.3 50.4 %copy-start.39 = (f32[1024]{0:T(1024)}, f32[1024]{0:T(1024)S(1)}, u32[]{:S(2)}) copy-start(f32[1024]{0:T(1024)S(1)} %broadcast_multiply_fusion.1) | copy-start | bytes 12292
  91.1 49.6 %copy-start.47 = (f32[1024]{0:T(1024)}, f32[1024]{0:T(1024)S(1)}, u32[]{:S(2)}) copy-start(f32[1024]{0:T(1024)S(1)} %add_rsqrt_fusion.1) | copy-start | bytes 12292
  140.7 16.8 %copy-start.7 = (bf16[1024,864]{0,1:T(8,128)(2,1)}, bf16[1024,864]{0,1:T(8,128)(2,1)S(1)}, u32[]{:S(2)}) copy-start(bf16[1024,864]{0,1:T(8,128)(2,1)S(1)} %add_convert_fusion.1) | copy-start | bytes 5308420
  157.5 8.6 copy-start.37
  157.6 8.6 copy-start.31
  166.1 36.6 %copy-start.58 = (bf16[1152]{0:T(1024)(128)(2,1)S(1)}, bf16[1152]{0:T(1024)(128)(2,1)}, u32[]{:S(2)}) copy-start(bf16[1152]{0:T(1024)(128)(2,1)} %param.26) | copy-start | bytes 6916
  166.1 117.2 %all-gather.27.cloned.1.call-start = ((), (), s32[]{:S(2)}) async-start(), calls=%async_computation.9 | async-start | bytes 3317760 | tf_op jit(solution)/shard_map/all_gather | solution.py:149
  201.2 139.2 %all-gather.29.cloned.1.call-start = ((), (), s32[]{:S(2)}) async-start(), calls=%async_computation.10 | async-start | bytes 3317760 | tf_op jit(solution)/shard_map/all_gather | solution.py:150
  201.9 197.9 %reduce-scatter.10.cloned.1.call-start = ((), (), s32[]{:S(2)}) async-start(), calls=%async_computation.12 | async-start | bytes 3932160 | tf_op jit(solution)/shard_map/reduce_scatter | solution.py:47
  208.0 138.5 %copy-start.18 = (bf16[1152,288]{0,1:T(8,128)(2,1)}, bf16[1152,288]{0,1:T(8,128)(2,1)S(1)}, u32[]{:S(2)}) copy-start(bf16[1152,288]{0,1:T(8,128)(2,1)S(1)} %get-tuple-element.94) | copy-start | bytes 1990660
  208.0 138.5 %copy-start.20 = (bf16[1152,288]{0,1:T(8,128)(2,1)}, bf16[1152,288]{0,1:T(8,128)(2,1)S(1)}, u32[]{:S(2)}) copy-start(bf16[1152,288]{0,1:T(8,128)(2,1)S(1)} %get-tuple-element.95) | copy-start | bytes 1990660
  208.0 138.5 %copy-start.21 = (bf16[1152,288]{0,1:T(8,128)(2,1)}, bf16[1152,288]{0,1:T(8,128)(2,1)S(1)}, u32[]{:S(2)}) copy-start(bf16[1152,288]{0,1:T(8,128)(2,1)S(1)} %get-tuple-element.96) | copy-start | bytes 1990660
  232.6 50.8 %copy-start.34 = (f32[1152]{0:T(1024)S(1)}, f32[1152]{0:T(1024)}, u32[]{:S(2)}) copy-start(f32[1152]{0:T(1024)} %get-tuple-element.70) | copy-start | bytes 13828
  283.4 7.6 copy-start.2
  291.0 62.9 %copy-start.32 = (f32[1024]{0:T(1024)}, f32[1024]{0:T(1024)S(1)}, u32[]{:S(2)}) copy-start(f32[1024]{0:T(1024)S(1)} %broadcast_multiply_fusion) | copy-start | bytes 12292
  292.1 61.9 %copy-start.35 = (f32[1024]{0:T(1024)}, f32[1024]{0:T(1024)S(1)}, u32[]{:S(2)}) copy-start(f32[1024]{0:T(1024)S(1)} %add_rsqrt_fusion) | copy-start | bytes 12292
  295.7 50.8 %copy-start.53 = (f32[1152]{0:T(1024)S(1)}, f32[1152]{0:T(1024)}, u32[]{:S(2)}) copy-start(f32[1152]{0:T(1024)} %get-tuple-element.67) | copy-start | bytes 13828
  340.4 13.6 %slice-start = ((s8[4718592]{0:T(1024)(128)(4,1)}), s8[4194304]{0:T(1024)(128)(4,1)S(1)}, s32[]{:S(2)}) async-start(s8[4718592]{0:T(1024)(128)(4,1)} %bitcast.202), calls=%async_computation.24 | async-start | bytes 8388608
  346.5 7.5 copy-start.68
  346.6 7.4 copy-start.3
  346.6 7.4 slice-start.1
  346.6 7.4 copy-start.67
  362.7 92.2 %reduce-scatter.20.cloned.1.call-start = ((), (), s32[]{:S(2)}) async-start(), calls=%async_computation.18 | async-start | bytes 3317760 | tf_op jit(solution)/shard_map/reduce_scatter | solution.py:53
  372.4 8.0 copy-start.15
  372.4 137.8 %reduce-scatter.18.cloned.1.call-start = ((), (), s32[]{:S(2)}) async-start(), calls=%async_computation.16 | async-start | bytes 3317760 | tf_op jit(solution)/shard_map/reduce_scatter | solution.py:53
  379.6 20.2 %copy-start.6 = (bf16[1024,288]{1,0:T(8,128)(2,1)S(1)}, bf16[1024,288]{1,0:T(8,128)(2,1)}, u32[]{:S(2)}) copy-start(bf16[1024,288]{1,0:T(8,128)(2,1)} %copy.51) | copy-start | bytes 1769476
  379.7 161.0 %all-gather.41.cloned.1.call-start = ((), (), s32[]{:S(2)}) async-start(), calls=%async_computation.23 | async-start | bytes 3932160 | tf_op jit(solution)/shard_map/all_gather | solution.py:39
  380.7 23.5 %copy-start.10 = (bf16[1024,288]{1,0:T(8,128)(2,1)}, bf16[1024,288]{1,0:T(8,128)(2,1)S(1)}, u32[]{:S(2)}) copy-start(bf16[1024,288]{1,0:T(8,128)(2,1)S(1)} %copy.58) | copy-start | bytes 1769476
  399.9 55.1 %copy-start.38 = (f32[4,1024]{1,0:T(4,128)S(1)}, f32[4,1024]{1,0:T(4,128)}, u32[]{:S(2)}) copy-start(f32[4,1024]{1,0:T(4,128)} %copy-done.37) | copy-start | bytes 49156
  404.2 225.2 %all-gather.33.cloned.1.call-start = ((), (), s32[]{:S(2)}) async-start(), calls=%async_computation.19 | async-start | bytes 1990656 | tf_op jit(solution)/shard_map/all_gather | solution.py:56
  455.0 177.1 %all-gather.31.cloned.1.call-start = ((), (), s32[]{:S(2)}) async-start(), calls=%async_computation.17 | async-start | bytes 1990656 | tf_op jit(solution)/shard_map/all_gather | solution.py:56
  510.2 157.0 %reduce-scatter.16.cloned.1.call-start = ((), (), s32[]{:S(2)}) async-start(), calls=%async_computation.15 | async-start | bytes 1105920 | tf_op jit(solution)/shard_map/reduce_scatter | solution.py:53
  574.0 101.7 %reduce-scatter.14.cloned.1.call-start = ((), (), s32[]{:S(2)}) async-start(), calls=%async_computation.14 | async-start | bytes 2580480 | tf_op jit(solution)/shard_map/reduce_scatter | solution.py:53
  574.0 12.9 %copy-start.8 = (bf16[1024,864]{0,1:T(8,128)(2,1)S(1)}, bf16[1024,864]{0,1:T(8,128)(2,1)}, u32[]{:S(2)}) copy-start(bf16[1024,864]{0,1:T(8,128)(2,1)} %copy-done.7) | copy-start | bytes 5308420
  589.6 10.6 %copy-start.11 = (bf16[4,72,1024]{2,1,0:T(8,128)(2,1)}, bf16[4,72,1024]{2,1,0:T(8,128)(2,1)S(1)}, u32[]{:S(2)}) copy-start(bf16[4,72,1024]{2,1,0:T(8,128)(2,1)S(1)} %fusion.50) | copy-start | bytes 1769476
  600.2 106.0 %reduce-scatter.12.cloned.1.call-start = ((), (), s32[]{:S(2)}) async-start(), calls=%async_computation.13 | async-start | bytes 3932160 | tf_op jit(solution)/shard_map/reduce_scatter | solution.py:47
  610.1 136.5 %reduce-scatter.8.cloned.1.call-start = ((), (), s32[]{:S(2)}) async-start(), calls=%async_computation.11 | async-start | bytes 3932160 | tf_op jit(solution)/shard_map/reduce_scatter | solution.py:47
  621.7 7.4 copy-start.9
  660.2 32.3 %copy-start.45 = (f32[1728]{0:T(1024)}, f32[1728]{0:T(1024)S(1)}, u32[]{:S(2)}) copy-start(f32[1728]{0:T(1024)S(1)} %psum.31) | copy-start | bytes 20740
  689.8 56.9 %copy-start.33 = (f32[1024]{0:T(1024)S(1)}, f32[1024]{0:T(1024)}, u32[]{:S(2)}) copy-start(f32[1024]{0:T(1024)} %copy-done.32) | copy-start | bytes 12292
  689.8 56.9 %copy-start.36 = (f32[1024]{0:T(1024)S(1)}, f32[1024]{0:T(1024)}, u32[]{:S(2)}) copy-start(f32[1024]{0:T(1024)} %copy-done.35) | copy-start | bytes 12292
  689.8 56.9 %copy-start.46 = (f32[288]{0:T(512)S(1)}, f32[288]{0:T(512)}, u32[]{:S(2)}) copy-start(f32[288]{0:T(512)} %get-tuple-element.66) | copy-start | bytes 3460
  689.8 56.9 %copy-start.55 = (f32[288]{0:T(512)S(1)}, f32[288]{0:T(512)}, u32[]{:S(2)}) copy-start(f32[288]{0:T(512)} %get-tuple-element.63) | copy-start | bytes 3460
  689.8 56.9 %copy-start.56 = (f32[288]{0:T(512)S(1)}, f32[288]{0:T(512)}, u32[]{:S(2)}) copy-start(f32[288]{0:T(512)} %get-tuple-element.65) | copy-start | bytes 3460
  834.2 67.1 %collective-permute-start.3 = (bf16[1024,288]{0,1:T(8,128)(2,1)}, bf16[1024,288]{0,1:T(8,128)(2,1)S(1)}, u32[]{:S(2)}, u32[]{:S(2)}) collective-permute-start(bf16[1024,288]{0,1:T(8,128)(2,1)} %copy.62), channel_id=1, source_target_pairs={{0,0},{1,4},{2,8},{3,12},{4,1},{5,5},{6,9},{7,13},{8,2},{9,6},{10,... | collective-permute-start | bytes 1769480 | tf_op jit(solution)/shard_map/ppermute | solution.py:31
  835.9 66.5 %collective-permute-start.1 = (bf16[1024,288]{0,1:T(8,128)(2,1)S(1)}, bf16[1024,288]{0,1:T(8,128)(2,1)S(1)}, u32[]{:S(2)}, u32[]{:S(2)}) collective-permute-start(bf16[1024,288]{0,1:T(8,128)(2,1)S(1)} %copy.57), channel_id=1, source_target_pairs={{0,0},{1,4},{2,8},{3,12},{4,1},{5,5},{6,9},{7,13},{8,2},{9,6},{10,... | collective-permute-start | bytes 1769480 | tf_op jit(solution)/shard_map/ppermute | solution.py:31
  (29 other events, 87.9 us)
Sparse Core Ops, SparseCore 0:
  10.5 68.8 all-gather.34
  81.5 54.0 all-gather.22
  137.1 68.0 all-gather.36
  206.7 22.8 all-gather.38
  231.5 24.0 all-gather.24
  257.6 25.7 all-gather.26
  285.0 55.3 all-gather.28
  362.9 36.9 reduce-scatter.9
  402.3 52.6 reduce-scatter.19
  457.8 52.3 reduce-scatter.17
  512.4 28.2 all-gather.40
  542.1 24.4 all-gather.32
  568.2 24.4 all-gather.30
  595.5 24.5 reduce-scatter.15
  623.0 43.4 reduce-scatter.13
  668.9 37.1 reduce-scatter.11
  708.7 37.9 reduce-scatter.7

commit v2 on v1

--- a/solution.py
+++ b/solution.py
@@ -53,6 +53,9 @@
     piece = lax.psum_scatter(
         blocks.astype(jnp.bfloat16), "row", scatter_dimension=0, tiled=False
     )
+    if lax.axis_size("dp") == 2:
+        other = lax.ppermute(piece, "dp", [(0, 1), (1, 0)])
+        return piece.astype(jnp.float32) + other.astype(jnp.float32)
     both = lax.all_gather(piece, "dp", axis=0).astype(jnp.float32)
     return jnp.sum(both, axis=0)
 

time: 911 us -> 859 us (0.943)
  waiting for transfers between devices: 363 us -> 318 us
  blocking collectives: 288 us -> 263 us
  matrix products: 114 us -> 127 us
    reduce_scatter x4, waiting for transfers between devices: 106 us -> 30.3 us  [grad_sum(): lax.psum_scatter(blocks.astype(jnp.bfloat16), 'row', scatter_dimension=0,...]
    reduce_scatter x3, waiting for transfers between devices: 60.8 us -> 88.8 us  [sum_scatter(): lax.psum_scatter(blocks.astype(jnp.bfloat16), axis_name, scatter_dimensio...]
    ppermute x0 -> x4, waiting for transfers between devices: none -> 20.9 us  [grad_sum(): other = lax.ppermute(piece, 'dp', [(0, 1), (1, 0)])]
    all_gather x2 -> x0, blocking collectives: 20.7 us -> none  [grad_sum(): both = lax.all_gather(piece, 'dp', axis=0).astype(jnp.float32)]
    all_gather x5, waiting for transfers between devices: 81 us -> 62.8 us  [gather_wide(): return side_by_side(lax.all_gather(value, axis_name, axis=0))]
  transfers between devices with their start and end apart: 21 -> 23, of which waited for: 13 -> 16; matrix products, arithmetic and copies ran while one was open for 22% -> 24% of each run, Pallas kernels for 0% -> 0%
where the time goes in v2:
time: 859 us; the launch traced here: 858 us
  waiting for transfers between devices  318 us (37%)
  blocking collectives  263 us (31%)
  matrix products  127 us (15%)
  local copies, waits for them, and re-layouts  61.4 us (7%)
  other arithmetic  59 us (7%)
  between operations  15 us (2%)
  starting transfers between devices  13.7 us (2%)
    reduce_scatter x3, waiting for transfers between devices, sum_scatter(): lax.psum_scatter(blocks.astype(jnp.bfloat16), axis_name, scatter_dimensio...  88.8 us
    all_gather x2, blocking collectives, every_latent(): full = lax.all_gather(part, ('dp', 'row', 'col'), axis=0)  78.5 us
    dot_general x12, matrix products, matmul(): lax.dot_general(left, right, (((left_dim,), (right_dim,)), ((), ())), pre...  71 us
    all_gather x5, waiting for transfers between devices, gather_wide(): return side_by_side(lax.all_gather(value, axis_name, axis=0))  62.8 us
    psum x1, blocking collectives, per_device(): d_activated = lax.psum(d_activated, 'row')  57.8 us
    all_gather x1, blocking collectives, per_device(): lax.all_gather(packed, ('row', 'col'), axis=0)  56 us
    all_gather x1, waiting for transfers between devices, per_device(): w_fc1_all = lax.all_gather(w_fc1, 'row', axis=0, tiled=True)  44.7 us
    all_gather x1, waiting for transfers between devices, per_device(): w_qkv_all = lax.all_gather(w_qkv, 'row', axis=0, tiled=True)  44.5 us
  transfers between devices with their start and end apart: 23, of which 16 were waited for; matrix products, arithmetic and copies ran while one was open for 24% of the time, Pallas kernels for 0%

profile of v2, /device:TPU:0, one launch (start us, length us, event | category | flops | bytes accessed | tf_op | source)
XLA Modules:
  0.0 857.7 jit_solution(5195239682034047490)
XLA Ops:
  16.9 56.0 %all-gather.8 = f32[16,26,288]{2,1,0:T(8,128)S(1)} all-gather(f32[1,26,288]{2,1,0:T(8,128)S(1)} %maximum_bitcast_fusion), channel_id=2, replica_groups=mesh['dp'=2,'row'=4,'col'=4] {'row','col'}, dimensions={0}, use_global_device_ids=true | all-gather | bytes 509184 | tf_op jit(solution)/shard_map/all_gather | solution.py:172
  75.6 3.7 all-gather.29.cloned.1.call-done
  79.3 3.3 fusion.102
  82.6 5.3 concatenate.48
  87.9 2.2 convert_reduce_fusion
  91.1 44.5 %all-gather.21.cloned.1.call-done = bf16[1152,864]{1,0:T(8,128)(2,1)} async-done(((bf16[288,864]{1,0:T(8,128)(2,1)}), bf16[1152,864]{1,0:T(8,128)(2,1)}) %all-gather.21.cloned.1.call-update) | async-done | bytes 1990672 | tf_op jit(solution)/shard_map/all_gather | solution.py:150
  135.6 5.1 add_convert_fusion.1
  140.7 8.2 multiply_reduce_fusion.1
  149.0 8.6 %fusion = f32[4,1024]{1,0:T(4,128)S(1)} fusion(f32[4,1024,1024]{1,2,0:T(8,128)} %get-tuple-element.149, f32[4,1024]{1,0:T(4,128)S(1)} %get-tuple-element.148), kind=kLoop, calls=%fused_computation.5 | loop fusion | flops 12578816 | bytes 16809984 | tf_op jit(solution)/shard_map/reduce_sum | solution.py:76
  157.6 8.5 fusion.54
  166.2 33.6 %all-gather.2 = bf16[1152,288]{1,0:T(8,128)(2,1)S(1)} all-gather(bf16[288,288]{1,0:T(8,128)(2,1)S(1)} %copy-done.29), channel_id=4, replica_groups=mesh['dp'=2,'row'=4,'col'=4] {'row'}, dimensions={0}, use_global_device_ids=true | all-gather | bytes 829440 | tf_op jit(solution)/shard_map/all_gather | solution.py:39
  202.9 2.3 all-gather.31.cloned.1.call-done
  205.3 2.7 fusion.103
  208.0 21.5 %all-gather.33.cloned.1.call-done = bf16[4096,288]{0,1:T(8,128)(2,1)} async-done(((bf16[1024,288]{0,1:T(8,128)(2,1)}), bf16[4096,288]{0,1:T(8,128)(2,1)}) %all-gather.33.cloned.1.call-update) | async-done | bytes 2359312 | tf_op jit(solution)/shard_map/all_gather | solution.py:39
  229.5 3.1 fusion.104
  232.6 23.0 %all-gather.23.cloned.1.call-done = bf16[4,1024,288]{1,2,0:T(8,128)(2,1)} async-done(((bf16[1,1024,288]{1,2,0:T(8,128)(2,1)}), bf16[4,1024,288]{1,2,0:T(8,128)(2,1)}) %all-gather.23.cloned.1.call-update) | async-done | bytes 2359312 | tf_op jit(solution)/shard_map/all_gather | solution.py:39
  255.6 3.1 slice_bitcast_fusion.19
  258.7 24.7 %all-gather.25.cloned.1.call-done = bf16[1152,1152]{1,0:T(8,128)(2,1)} async-done(((bf16[288,1152]{1,0:T(8,128)(2,1)}), bf16[1152,1152]{1,0:T(8,128)(2,1)}) %all-gather.25.cloned.1.call-update) | async-done | bytes 2654224 | tf_op jit(solution)/shard_map/all_gather | solution.py:152
  283.4 7.6 fusion.98
  293.2 2.4 add_convert_fusion
  295.7 44.7 %all-gather.27.cloned.1.call-done = bf16[1152,1152]{1,0:T(8,128)(2,1)} async-done(((bf16[288,1152]{1,0:T(8,128)(2,1)}), bf16[1152,1152]{1,0:T(8,128)(2,1)}) %all-gather.27.cloned.1.call-update) | async-done | bytes 2654224 | tf_op jit(solution)/shard_map/all_gather | solution.py:153
  340.4 6.1 convolution_add_fusion
  346.6 7.3 convert_reduce_fusion.1
  354.0 4.7 multiply_reduce_fusion.5
  364.2 7.0 psum.28
  371.2 27.7 %reduce-scatter.10.cloned.1.call-done = bf16[1,1024,288]{2,1,0:T(8,128)(2,1)} async-done(((bf16[4,1024,288]{2,1,0:T(8,128)(2,1)}), bf16[1,1024,288]{2,1,0:T(8,128)(2,1)}) %reduce-scatter.10.cloned.1.call-update) | async-done | bytes 589840 | tf_op jit(solution)/shard_map/reduce_scatter | solution.py:47
  398.9 4.0 convert_reduce_fusion.6
  403.1 7.2 convolution_convert_fusion.1
  410.4 7.0 convolution_convert_fusion
  419.5 12.2 %all-gather.35.cloned.1.call-done = bf16[4096,288]{1,0:T(8,128)(2,1)} async-done(((bf16[1024,288]{1,0:T(8,128)(2,1)}), bf16[4096,288]{1,0:T(8,128)(2,1)}) %all-gather.35.cloned.1.call-update) | async-done | bytes 2359312 | tf_op jit(solution)/shard_map/all_gather | solution.py:39
  431.7 3.3 fusion.101
  435.0 5.8 concatenate.56
  440.8 3.6 convolution_convert_fusion.5
  444.4 14.2 %multiply_reduce_fusion = (f32[4,1024]{1,0:T(4,128)S(1)}, f32[4,1024,1024]{1,2,0:T(8,128)}) fusion(f32[4,1024,1024]{1,2,0:T(8,128)} %get-tuple-element.149, f32[4,1024]{1,0:T(4,128)S(1)} %log_add_fusion, bf16[1024,4,72]{0,2,1:T(8,128)(2,1)} %bitcast.232, bf16[1024,3,4,72]{0,3,2,1:T(8,128)(2,1)} %bitcast.217), kind=kOutput, calls=%fused_computation.1 | convolution fusion | flops 620752896 | bytes 34766848 | tf_op jit(solution)/shard_map/qhe,khe->hqk/dot_general | solution.py:89
  461.3 10.9 %multiply_convert_fusion = bf16[4,1024,1024]{1,2,0:T(8,128)(2,1)} fusion(f32[4,1024,1024]{1,2,0:T(8,128)} %get-tuple-element.154, f32[4,1024,1024]{1,2,0:T(8,128)S(1)} %bitcast.211, f32[4,1024]{1,0:T(4,128)S(1)} %get-tuple-element.153, f32[4,1024]{1,0:T(4,128)S(1)} %log_add_fusion), kind=kLoop, calls=%fused_computation | loop fusion | flops 20971520 | bytes 41975808 | tf_op jit(solution)/shard_map/convert_element_type | solution.py:91
  472.2 6.9 fusion.50
  479.1 5.9 fusion.49
  484.9 4.9 fusion.51
  489.9 6.2 convolution_convert_fusion.3
  496.1 4.2 copy.67
  500.7 2.6 convolution_convert_fusion.4
  504.9 6.4 multiply_reduce_fusion.4
  515.8 7.1 convolution_convert_fusion.2
  524.2 2.1 pad_maximum_fusion
  526.9 4.2 all-gather.9
  535.2 6.8 reduce-scatter.20.cloned.1.call-done
  543.7 5.7 collective-permute-done.6
  549.4 2.6 convert_add_fusion.5
  552.1 9.9 %collective-permute-done.7 = bf16[1152,288]{0,1:T(8,128)(2,1)S(1)} collective-permute-done((bf16[1152,288]{0,1:T(8,128)(2,1)}, bf16[1152,288]{0,1:T(8,128)(2,1)S(1)}, u32[]{:S(2)}, u32[]{:S(2)}) %collective-permute-start.7) | collective-permute-done | bytes 663584 | tf_op jit(solution)/shard_map/ppermute | solution.py:57
  563.6 23.5 %reduce-scatter.14.cloned.1.call-done = bf16[1,288,864]{2,1,0:T(8,128)(2,1)} async-done(((bf16[4,288,864]{2,1,0:T(8,128)(2,1)}), bf16[1,288,864]{2,1,0:T(8,128)(2,1)}) %reduce-scatter.14.cloned.1.call-update) | async-done | bytes 497680 | tf_op jit(solution)/shard_map/reduce_scatter | solution.py:53
  588.7 19.7 %psum.31 = f32[1728]{0:T(1024)S(1)} all-reduce(f32[1728]{0:T(1024)S(1)} %concatenate.60), channel_id=1, replica_groups=mesh['dp'=2,'row'=4,'col'=4] {'dp','row'}, use_global_device_ids=true, to_apply=%region_30.31 | all-reduce | flops 1728 | bytes 13824 | tf_op jit(solution)/shard_map/psum | solution.py:270
  609.1 6.1 psum.29
  617.1 5.3 collective-permute-done.5
  624.1 2.2 convert_add_fusion.6
  626.4 2.7 copy.68
  629.1 2.9 copy.69
  632.0 21.8 %reduce-scatter.12.cloned.1.call-done = bf16[1,1024,288]{2,1,0:T(8,128)(2,1)} async-done(((bf16[4,1024,288]{2,1,0:T(8,128)(2,1)}), bf16[1,1024,288]{2,1,0:T(8,128)(2,1)}) %reduce-scatter.12.cloned.1.call-update) | async-done | bytes 589840 | tf_op jit(solution)/shard_map/reduce_scatter | solution.py:47
  655.1 39.2 %reduce-scatter.8.cloned.1.call-done = bf16[1,1024,288]{2,1,0:T(8,128)(2,1)} async-done(((bf16[4,1024,288]{2,1,0:T(8,128)(2,1)}), bf16[1,1024,288]{2,1,0:T(8,128)(2,1)}) %reduce-scatter.8.cloned.1.call-update) | async-done | bytes 589840 | tf_op jit(solution)/shard_map/reduce_scatter | solution.py:47
  694.4 5.3 fusion.41
  699.8 40.8 %all-gather.10 = f32[32,2,288]{2,1,0:T(2,128)S(1)} all-gather(f32[1,2,288]{2,1,0:T(2,128)S(1)} %maximum_bitcast_fusion.1), channel_id=8, replica_groups=mesh['dp'=2,'row'=4,'col'=4] {'dp','row','col'}, dimensions={0}, use_global_device_ids=true | all-gather | bytes 76032 | tf_op jit(solution)/shard_map/all_gather | solution.py:249
  740.6 37.7 %all-gather.11 = f32[32,6,288]{2,1,0:T(8,128)S(1)} all-gather(f32[1,6,288]{2,1,0:T(8,128)S(1)} %bitcast.250), channel_id=9, replica_groups=mesh['dp'=2,'row'=4,'col'=4] {'dp','row','col'}, dimensions={0}, use_global_device_ids=true | all-gather | bytes 228096 | tf_op jit(solution)/shard_map/all_gather | solution.py:249
  779.8 2.2 copy.63
  786.7 57.8 %psum.30 = f32[8,288]{1,0:T(8,128)S(1)} all-reduce(f32[8,288]{1,0:T(8,128)S(1)} %convolution_bitcast_fusion), channel_id=1, replica_groups=mesh['dp'=2,'row'=4,'col'=4] {'row'}, use_global_device_ids=true, to_apply=%region_25.26 | all-reduce | flops 2304 | bytes 18432 | tf_op jit(solution)/shard_map/psum | solution.py:265
  846.3 2.8 fusion.59
  (277 shorter events, 61.7 us)
Async XLA Ops:
  7.2 8.9 %copy-start = (bf16[288,6,288]{2,0,1:T(8,128)(2,1)S(1)}, bf16[288,6,288]{2,0,1:T(8,128)(2,1)}, u32[]{:S(2)}) copy-start(bf16[288,6,288]{2,0,1:T(8,128)(2,1)} %param.19) | copy-start | bytes 2985988
  7.2 8.9 %copy-start.14 = (bf16[1000,288]{0,1:T(8,128)(2,1)S(1)}, bf16[1000,288]{0,1:T(8,128)(2,1)}, u32[]{:S(2)}) copy-start(bf16[1000,288]{0,1:T(8,128)(2,1)} %param.18) | copy-start | bytes 1728004
  7.2 8.8 %copy-start.55 = (s32[4]{0:T(128)S(1)}, s32[4]{0:T(128)}, u32[]{:S(2)}) copy-start(s32[4]{0:T(128)} %param.16) | copy-start | bytes 52
  7.3 72.1 %all-gather.29.cloned.1.call-start = ((), (), s32[]{:S(2)}) async-start(), calls=%async_computation.18 | async-start | bytes 3932160 | tf_op jit(solution)/shard_map/all_gather | solution.py:39
  7.3 1.9 collective-permute-start
  10.3 62.6 %copy-start.57 = (bf16[2,288]{1,0:T(2,128)(2,1)S(1)}, bf16[2,288]{1,0:T(2,128)(2,1)}, u32[]{:S(2)}) copy-start(bf16[2,288]{1,0:T(2,128)(2,1)} %param.22) | copy-start | bytes 3460
  10.4 125.2 %all-gather.21.cloned.1.call-start = ((), (), s32[]{:S(2)}) async-start(), calls=%async_computation.7 | async-start | bytes 2580480 | tf_op jit(solution)/shard_map/all_gather | solution.py:150
  12.9 192.3 %all-gather.31.cloned.1.call-start = ((), (), s32[]{:S(2)}) async-start(), calls=%async_computation.19 | async-start | bytes 3317760 | tf_op jit(solution)/shard_map/all_gather | solution.py:39
  13.7 215.9 %all-gather.33.cloned.1.call-start = ((), (), s32[]{:S(2)}) async-start(), calls=%async_computation.20 | async-start | bytes 2949120 | tf_op jit(solution)/shard_map/all_gather | solution.py:39
  13.7 60.8 %collective-permute-start.2 = (bf16[1024,288]{0,1:T(8,128)(2,1)}, bf16[1024,288]{0,1:T(8,128)(2,1)S(1)}, u32[]{:S(2)}, u32[]{:S(2)}) collective-permute-start(bf16[1024,288]{0,1:T(8,128)(2,1)} %param.29), channel_id=1, source_target_pairs={{0,0},{1,4},{2,8},{3,12},{4,1},{5,5},{6,9},{7,13},{8,2},{9,6},{10,... | collective-permute-start | bytes 1769480 | tf_op jit(solution)/shard_map/ppermute | solution.py:31
  74.5 66.2 %copy-start.43 = (f32[1152]{0:T(1024)}, f32[1152]{0:T(1024)S(1)}, u32[]{:S(2)}) copy-start(f32[1152]{0:T(1024)S(1)} %get-tuple-element.72) | copy-start | bytes 13828
  75.4 180.3 %all-gather.23.cloned.1.call-start = ((), (), s32[]{:S(2)}) async-start(), calls=%async_computation.8 | async-start | bytes 2949120 | tf_op jit(solution)/shard_map/all_gather | solution.py:39
  87.9 47.6 %copy-start.45 = (f32[1152]{0:T(1024)S(1)}, f32[1152]{0:T(1024)}, u32[]{:S(2)}) copy-start(f32[1152]{0:T(1024)} %get-tuple-element.71) | copy-start | bytes 13828
  87.9 47.6 %copy-start.54 = (f32[864]{0:T(1024)S(1)}, f32[864]{0:T(1024)}, u32[]{:S(2)}) copy-start(f32[864]{0:T(1024)} %pad_maximum_fusion.16) | copy-start | bytes 10372
  90.3 414.5 %copy-start.32 = (f32[1024]{0:T(1024)}, f32[1024]{0:T(1024)S(1)}, u32[]{:S(2)}) copy-start(f32[1024]{0:T(1024)S(1)} %broadcast_multiply_fusion.1) | copy-start | bytes 12292
  91.1 413.8 %copy-start.41 = (f32[1024]{0:T(1024)}, f32[1024]{0:T(1024)S(1)}, u32[]{:S(2)}) copy-start(f32[1024]{0:T(1024)S(1)} %add_rsqrt_fusion.1) | copy-start | bytes 12292
  140.7 16.9 %copy-start.6 = (bf16[1024,864]{0,1:T(8,128)(2,1)}, bf16[1024,864]{0,1:T(8,128)(2,1)S(1)}, u32[]{:S(2)}) copy-start(bf16[1024,864]{0,1:T(8,128)(2,1)S(1)} %add_convert_fusion.1) | copy-start | bytes 5308420
  157.6 8.6 %copy-start.29 = (bf16[288,288]{1,0:T(8,128)(2,1)S(1)}, bf16[288,288]{1,0:T(8,128)(2,1)}, u32[]{:S(2)}) copy-start(bf16[288,288]{1,0:T(8,128)(2,1)} %param.23) | copy-start | bytes 497668
  166.1 36.6 %copy-start.53 = (bf16[1152]{0:T(1024)(128)(2,1)S(1)}, bf16[1152]{0:T(1024)(128)(2,1)}, u32[]{:S(2)}) copy-start(bf16[1152]{0:T(1024)(128)(2,1)} %param.26) | copy-start | bytes 6916
  166.2 117.2 %all-gather.25.cloned.1.call-start = ((), (), s32[]{:S(2)}) async-start(), calls=%async_computation.9 | async-start | bytes 3317760 | tf_op jit(solution)/shard_map/all_gather | solution.py:152
  201.2 139.1 %all-gather.27.cloned.1.call-start = ((), (), s32[]{:S(2)}) async-start(), calls=%async_computation.10 | async-start | bytes 3317760 | tf_op jit(solution)/shard_map/all_gather | solution.py:153
  202.0 197.0 %reduce-scatter.10.cloned.1.call-start = ((), (), s32[]{:S(2)}) async-start(), calls=%async_computation.12 | async-start | bytes 3932160 | tf_op jit(solution)/shard_map/reduce_scatter | solution.py:47
  208.0 138.5 %copy-start.18 = (bf16[1152,288]{0,1:T(8,128)(2,1)}, bf16[1152,288]{0,1:T(8,128)(2,1)S(1)}, u32[]{:S(2)}) copy-start(bf16[1152,288]{0,1:T(8,128)(2,1)S(1)} %get-tuple-element.94) | copy-start | bytes 1990660
  208.0 138.5 %copy-start.20 = (bf16[1152,288]{0,1:T(8,128)(2,1)}, bf16[1152,288]{0,1:T(8,128)(2,1)S(1)}, u32[]{:S(2)}) copy-start(bf16[1152,288]{0,1:T(8,128)(2,1)S(1)} %get-tuple-element.95) | copy-start | bytes 1990660
  208.0 138.5 %copy-start.21 = (bf16[1152,288]{0,1:T(8,128)(2,1)}, bf16[1152,288]{0,1:T(8,128)(2,1)S(1)}, u32[]{:S(2)}) copy-start(bf16[1152,288]{0,1:T(8,128)(2,1)S(1)} %get-tuple-element.96) | copy-start | bytes 1990660
  292.1 106.8 %copy-start.30 = (f32[1024]{0:T(1024)}, f32[1024]{0:T(1024)S(1)}, u32[]{:S(2)}) copy-start(f32[1024]{0:T(1024)S(1)} %add_rsqrt_fusion) | copy-start | bytes 12292
  295.7 50.9 %copy-start.46 = (f32[1152]{0:T(1024)S(1)}, f32[1152]{0:T(1024)}, u32[]{:S(2)}) copy-start(f32[1152]{0:T(1024)} %get-tuple-element.67) | copy-start | bytes 13828
  340.4 13.6 %slice-start.4 = ((s8[4718592]{0:T(1024)(128)(4,1)}), s8[4194304]{0:T(1024)(128)(4,1)S(1)}, s32[]{:S(2)}) async-start(s8[4718592]{0:T(1024)(128)(4,1)} %bitcast.212), calls=%async_computation.26 | async-start | bytes 8388608
  362.0 36.9 %copy-start.5 = (bf16[1024,288]{1,0:T(8,128)(2,1)S(1)}, bf16[1024,288]{1,0:T(8,128)(2,1)}, u32[]{:S(2)}) copy-start(bf16[1024,288]{1,0:T(8,128)(2,1)} %copy.52) | copy-start | bytes 1769476
  362.1 69.6 %all-gather.35.cloned.1.call-start = ((), (), s32[]{:S(2)}) async-start(), calls=%async_computation.21 | async-start | bytes 3932160 | tf_op jit(solution)/shard_map/all_gather | solution.py:39
  362.7 40.2 %copy-start.39 = (f32[288]{0:T(512)}, f32[288]{0:T(512)S(1)}, u32[]{:S(2)}) copy-start(f32[288]{0:T(512)S(1)} %get-tuple-element.66) | copy-start | bytes 3460
  364.2 38.8 %copy-start.9 = (bf16[1024,288]{1,0:T(8,128)(2,1)}, bf16[1024,288]{1,0:T(8,128)(2,1)S(1)}, u32[]{:S(2)}) copy-start(bf16[1024,288]{1,0:T(8,128)(2,1)S(1)} %copy.59) | copy-start | bytes 1769476
  403.0 128.2 %reduce-scatter.18.cloned.1.call-start = ((), (), s32[]{:S(2)}) async-start(), calls=%async_computation.16 | async-start | bytes 3317760 | tf_op jit(solution)/shard_map/reduce_scatter | solution.py:53
  410.3 131.7 %reduce-scatter.20.cloned.1.call-start = ((), (), s32[]{:S(2)}) async-start(), calls=%async_computation.17 | async-start | bytes 3317760 | tf_op jit(solution)/shard_map/reduce_scatter | solution.py:53
  419.4 167.7 %reduce-scatter.14.cloned.1.call-start = ((), (), s32[]{:S(2)}) async-start(), calls=%async_computation.14 | async-start | bytes 2580480 | tf_op jit(solution)/shard_map/reduce_scatter | solution.py:53
  444.4 14.2 %slice-start = ((s8[16777216]{0:T(1024)(128)(4,1)}), s8[4194304]{0:T(1024)(128)(4,1)S(1)}, s32[]{:S(2)}) async-start(s8[16777216]{0:T(1024)(128)(4,1)} %bitcast.210), calls=%async_computation.22 | async-start | bytes 8388608
  444.4 14.2 %slice-start.1 = ((s8[16777216]{0:T(1024)(128)(4,1)}), s8[4194304]{0:T(1024)(128)(4,1)S(1)}, s32[]{:S(2)}) async-start(s8[16777216]{0:T(1024)(128)(4,1)} %bitcast.210), calls=%async_computation.23 | async-start | bytes 8388608
  444.4 15.7 %slice-start.2 = ((s8[16777216]{0:T(1024)(128)(4,1)}), s8[4194304]{0:T(1024)(128)(4,1)S(1)}, s32[]{:S(2)}) async-start(s8[16777216]{0:T(1024)(128)(4,1)} %bitcast.210), calls=%async_computation.24 | async-start | bytes 8388608
  444.4 16.9 %slice-start.3 = ((s8[16777216]{0:T(1024)(128)(4,1)}), s8[4194304]{0:T(1024)(128)(4,1)S(1)}, s32[]{:S(2)}) async-start(s8[16777216]{0:T(1024)(128)(4,1)} %bitcast.210), calls=%async_computation.25 | async-start | bytes 8388608
  461.3 10.9 %copy-start.7 = (bf16[1024,864]{0,1:T(8,128)(2,1)S(1)}, bf16[1024,864]{0,1:T(8,128)(2,1)}, u32[]{:S(2)}) copy-start(bf16[1024,864]{0,1:T(8,128)(2,1)} %copy-done.6) | copy-start | bytes 5308420
  500.3 115.0 %reduce-scatter.16.cloned.1.call-start = ((), (), s32[]{:S(2)}) async-start(), calls=%async_computation.15 | async-start | bytes 1105920 | tf_op jit(solution)/shard_map/reduce_scatter | solution.py:53
  504.8 149.0 %reduce-scatter.12.cloned.1.call-start = ((), (), s32[]{:S(2)}) async-start(), calls=%async_computation.13 | async-start | bytes 3932160 | tf_op jit(solution)/shard_map/reduce_scatter | solution.py:47
  514.7 179.7 %reduce-scatter.8.cloned.1.call-start = ((), (), s32[]{:S(2)}) async-start(), calls=%async_computation.11 | async-start | bytes 3932160 | tf_op jit(solution)/shard_map/reduce_scatter | solution.py:47
  526.3 17.2 %copy-start.8 = (bf16[1,1024,288]{2,1,0:T(8,128)(2,1)S(1)}, bf16[1,1024,288]{2,1,0:T(8,128)(2,1)}, u32[]{:S(2)}) copy-start(bf16[1,1024,288]{2,1,0:T(8,128)(2,1)} %reduce-scatter.10.cloned.1.call-done) | copy-start | bytes 1769476
  531.3 18.2 %collective-permute-start.6 = (bf16[288,1152]{1,0:T(8,128)(2,1)}, bf16[288,1152]{1,0:T(8,128)(2,1)}, u32[]{:S(2)}, u32[]{:S(2)}) collective-permute-start(bf16[288,1152]{1,0:T(8,128)(2,1)} %bitcast.237), channel_id=1, source_target_pairs={{0,16},{16,0},{1,17},{17,1},{2,18},{18,2},{3,19},{19,3},{4,20},{20... | collective-permute-start | bytes 1990664 | tf_op jit(solution)/shard_map/ppermute | solution.py:57
  532.8 30.4 %copy-start.51 = (s32[8]{0:T(128)}, s32[8]{0:T(128)S(1)}, u32[]{:S(2)}) copy-start(s32[8]{0:T(128)S(1)} %get-tuple-element.147) | copy-start | bytes 100
  541.9 20.1 %copy-start.17 = (bf16[1,1152,288]{1,2,0:T(8,128)(2,1)S(1)}, bf16[1,1152,288]{1,2,0:T(8,128)(2,1)}, u32[]{:S(2)}) copy-start(bf16[1,1152,288]{1,2,0:T(8,128)(2,1)} %reduce-scatter.20.cloned.1.call-done) | copy-start | bytes 1990660
  542.0 21.3 %copy-start.11 = (bf16[4,72,1024]{2,1,0:T(8,128)(2,1)S(1)}, bf16[4,72,1024]{2,1,0:T(8,128)(2,1)}, u32[]{:S(2)}) copy-start(bf16[4,72,1024]{2,1,0:T(8,128)(2,1)} %fusion.50) | copy-start | bytes 1769476
  542.0 21.3 %copy-start.12 = (bf16[4,72,1024]{2,1,0:T(8,128)(2,1)S(1)}, bf16[4,72,1024]{2,1,0:T(8,128)(2,1)}, u32[]{:S(2)}) copy-start(bf16[4,72,1024]{2,1,0:T(8,128)(2,1)} %fusion.49) | copy-start | bytes 1769476
  542.0 21.3 %copy-start.13 = (bf16[4,72,1024]{2,1,0:T(8,128)(2,1)S(1)}, bf16[4,72,1024]{2,1,0:T(8,128)(2,1)}, u32[]{:S(2)}) copy-start(bf16[4,72,1024]{2,1,0:T(8,128)(2,1)} %fusion.51) | copy-start | bytes 1769476
  542.0 20.0 %collective-permute-start.7 = (bf16[1152,288]{0,1:T(8,128)(2,1)}, bf16[1152,288]{0,1:T(8,128)(2,1)S(1)}, u32[]{:S(2)}, u32[]{:S(2)}) collective-permute-start(bf16[1152,288]{0,1:T(8,128)(2,1)} %bitcast.238), channel_id=1, source_target_pairs={{0,16},{16,0},{1,17},{17,1},{2,18},{18,2},{3,19},{19,3},{4,20},{20... | collective-permute-start | bytes 1990664 | tf_op jit(solution)/shard_map/ppermute | solution.py:57
  543.7 44.9 %copy-start.47 = (f32[1152]{0:T(1024)S(1)}, f32[1152]{0:T(1024)}, u32[]{:S(2)}) copy-start(f32[1152]{0:T(1024)} %get-tuple-element.156) | copy-start | bytes 13828
  587.1 37.0 %collective-permute-start.4 = (bf16[288,864]{1,0:T(8,128)(2,1)}, bf16[288,864]{1,0:T(8,128)(2,1)S(1)}, u32[]{:S(2)}, u32[]{:S(2)}) collective-permute-start(bf16[288,864]{1,0:T(8,128)(2,1)} %bitcast.242), channel_id=1, source_target_pairs={{0,16},{16,0},{1,17},{17,1},{2,18},{18,2},{3,19},{19,3},{4,20},{20... | collective-permute-start | bytes 1493000 | tf_op jit(solution)/shard_map/ppermute | solution.py:57
  608.5 23.6 %copy-start.38 = (f32[1728]{0:T(1024)}, f32[1728]{0:T(1024)S(1)}, u32[]{:S(2)}) copy-start(f32[1728]{0:T(1024)S(1)} %psum.31) | copy-start | bytes 20740
  615.2 7.1 collective-permute-start.5
  626.3 68.0 %copy-start.31 = (f32[1024]{0:T(1024)S(1)}, f32[1024]{0:T(1024)}, u32[]{:S(2)}) copy-start(f32[1024]{0:T(1024)} %copy-done.30) | copy-start | bytes 12292
  626.4 68.0 %copy-start.33 = (f32[1024]{0:T(1024)S(1)}, f32[1024]{0:T(1024)}, u32[]{:S(2)}) copy-start(f32[1024]{0:T(1024)} %copy-done.32) | copy-start | bytes 12292
  626.4 68.0 %copy-start.40 = (f32[288]{0:T(512)S(1)}, f32[288]{0:T(512)}, u32[]{:S(2)}) copy-start(f32[288]{0:T(512)} %copy-done.39) | copy-start | bytes 3460
  626.4 68.0 %copy-start.42 = (f32[1024]{0:T(1024)S(1)}, f32[1024]{0:T(1024)}, u32[]{:S(2)}) copy-start(f32[1024]{0:T(1024)} %copy-done.41) | copy-start | bytes 12292
  626.4 68.0 %copy-start.48 = (f32[288]{0:T(512)S(1)}, f32[288]{0:T(512)}, u32[]{:S(2)}) copy-start(f32[288]{0:T(512)} %get-tuple-element.63) | copy-start | bytes 3460
  626.4 68.0 %copy-start.49 = (f32[288]{0:T(512)S(1)}, f32[288]{0:T(512)}, u32[]{:S(2)}) copy-start(f32[288]{0:T(512)} %get-tuple-element.65) | copy-start | bytes 3460
  699.7 144.8 %copy-start.52 = (s32[8]{0:T(128)S(1)}, s32[8]{0:T(128)}, u32[]{:S(2)}) copy-start(s32[8]{0:T(128)} %copy-done.51) | copy-start | bytes 100
  782.0 67.1 %collective-permute-start.3 = (bf16[1024,288]{0,1:T(8,128)(2,1)}, bf16[1024,288]{0,1:T(8,128)(2,1)S(1)}, u32[]{:S(2)}, u32[]{:S(2)}) collective-permute-start(bf16[1024,288]{0,1:T(8,128)(2,1)} %copy.63), channel_id=1, source_target_pairs={{0,0},{1,4},{2,8},{3,12},{4,1},{5,5},{6,9},{7,13},{8,2},{9,6},{10,... | collective-permute-start | bytes 1769480 | tf_op jit(solution)/shard_map/ppermute | solution.py:31
  783.7 66.5 %collective-permute-start.1 = (bf16[1024,288]{0,1:T(8,128)(2,1)S(1)}, bf16[1024,288]{0,1:T(8,128)(2,1)S(1)}, u32[]{:S(2)}, u32[]{:S(2)}) collective-permute-start(bf16[1024,288]{0,1:T(8,128)(2,1)S(1)} %copy.58), channel_id=1, source_target_pairs={{0,0},{1,4},{2,8},{3,12},{4,1},{5,5},{6,9},{7,13},{8,2},{9,6},{10,... | collective-permute-start | bytes 1769480 | tf_op jit(solution)/shard_map/ppermute | solution.py:31
  (30 other events, 147.3 us)
Sparse Core Ops, SparseCore 0:
  10.5 68.8 all-gather.28
  81.5 54.0 all-gather.20
  137.1 68.0 all-gather.30
  206.7 22.8 all-gather.32
  231.5 24.0 all-gather.22
  257.6 25.7 all-gather.24
  285.0 55.3 all-gather.26
  362.2 36.6 reduce-scatter.9
  403.1 28.5 all-gather.34
  434.5 52.6 reduce-scatter.17
  489.6 52.3 reduce-scatter.19
  544.2 42.8 reduce-scatter.13
  590.0 24.5 reduce-scatter.15
  617.1 36.7 reduce-scatter.11
  656.4 37.9 reduce-scatter.7
